TPU v7x, 256 devices: a whole 4x4x8 slice. The times are simulated.
256 devices in a mesh: layer: 32 (over y, z), seq: 8 (over x, core).
Axes of the slice: x: 4, y: 4, z: 8, core: 2. Of those that a mesh axis runs over, the one named last changes fastest.
Arguments:
- states: bfloat16 [32, 1024, 1024], P('layer', 'seq'), may hold values from -8 to 8
- w_qkv: bfloat16 [32, 3, 1024, 512], P('layer'), may hold values from -0.1875 to 0.1875
- w_out: bfloat16 [32, 512, 1024], P('layer'), may hold values from -0.25 to 0.25
- norm_gain: float32 [32, 1024], P('layer'), may hold values from 0.25 to 1.75
- qk_gain: float32 [32, 2, 64], P('layer'), may hold values from 0.25 to 1.75
Outputs:
- corrected: bfloat16 [32, 1024, 1024], P('layer', 'seq')
All inputs are finite; a program needn't handle non-finite values.
Results may differ from a plain program's by a relative error of at most 0.034.
Values may be sent and summed in bfloat16 or wider, within the bound.
A program may use at most 64 MiB of HBM per device.

v0:
```python
import jax
import jax.numpy as jnp
from jax import lax
from jax.sharding import PartitionSpec as P

epsilon = 1e-06
step_size = 1.0


def from_behind(value, axis, by):
    size = lax.axis_size(axis)
    pairs = [(i, i + by) for i in range(size) if 0 <= i + by < size]
    return lax.ppermute(value, axis, pairs)


def normalize(state_rows, gain_vector):
    values_f = state_rows.astype(jnp.float32)
    inverse_rms = lax.rsqrt(jnp.mean(values_f * values_f, axis=-1, keepdims=True) + epsilon)
    return (values_f * inverse_rms * gain_vector).astype(jnp.bfloat16)


def head_norm(product, gain_vector):
    head_width = gain_vector.shape[-1]
    split_heads = product.reshape(product.shape[0], -1, head_width)
    inverse_rms = lax.rsqrt(jnp.mean(split_heads * split_heads, axis=-1, keepdims=True) + epsilon)
    return (split_heads * inverse_rms * gain_vector).astype(jnp.bfloat16)


def attend(queries, keys_all, values_all, positions, weight_out):
    head_width = queries.shape[-1]
    scores = jnp.einsum(
        "qhe,khe->hqk", queries, keys_all, preferred_element_type=jnp.float32
    ) * head_width ** (-0.5)
    key_positions = jnp.arange(keys_all.shape[0], dtype=jnp.int32)
    visible = key_positions[None, None, :] <= positions[None, :, None]
    weights = jnp.where(visible, jnp.exp(scores), 0.0)
    probabilities = (weights / jnp.sum(weights, axis=-1, keepdims=True)).astype(jnp.bfloat16)
    mixture = jnp.einsum(
        "hqk,khe->qhe", probabilities, values_all, preferred_element_type=jnp.float32
    ).astype(jnp.bfloat16)
    return jnp.dot(
        mixture.reshape(queries.shape[0], -1), weight_out, preferred_element_type=jnp.float32
    )


def exact_branch(state_rows, positions, gain_vector, weight_set, head_gains, weight_out):
    head_width = head_gains.shape[-1]
    normed = normalize(state_rows, gain_vector)
    queries = head_norm(
        jnp.dot(normed, weight_set[0], preferred_element_type=jnp.float32), head_gains[0]
    )
    key_rows = head_norm(
        jnp.dot(normed, weight_set[1], preferred_element_type=jnp.float32), head_gains[1]
    )
    value_rows = jnp.dot(normed, weight_set[2], preferred_element_type=jnp.float32).astype(
        jnp.bfloat16
    )
    key_flat = key_rows.reshape(key_rows.shape[0], -1)
    keys_all, values_all = (
        lax.all_gather(key_flat, "seq", axis=0, tiled=True),
        lax.all_gather(value_rows, "seq", axis=0, tiled=True),
    )
    keys_all = keys_all.reshape(keys_all.shape[0], -1, head_width)
    values_all = values_all.reshape(values_all.shape[0], -1, head_width)
    return (attend(queries, keys_all, values_all, positions, weight_out), keys_all, values_all)


def coarse_branch(
    state_rows,
    positions,
    groups,
    gain_vector,
    weight_query,
    query_gain,
    keys_all,
    values_all,
    weight_out,
):
    normed = normalize(state_rows, gain_vector)
    queries = head_norm(
        jnp.dot(normed, weight_query, preferred_element_type=jnp.float32), query_gain
    )
    pieces = []
    for first_row, last_row, key_count in groups:
        pieces.append(attend(queries, keys_all, values_all, positions, weight_out))
    return jnp.concatenate(pieces, axis=0)


def forward_hop(message):
    return from_behind(message, "layer", 1)


def on_device(states, w_qkv, w_out, norm_gain, qk_gain):
    start_state = states[0]
    weight_set = w_qkv[0]
    weight_out = w_out[0]
    gain_vector = norm_gain[0]
    head_gains = qk_gain[0]
    row_count = start_state.shape[0]
    seq_count = lax.axis_size("seq")
    seq_index = lax.axis_index("seq")
    layer_index = lax.axis_index("layer")
    pair_count = lax.axis_size("layer") // 2
    token_count = row_count * seq_count
    positions = seq_index * row_count + jnp.arange(row_count, dtype=jnp.int32)
    is_even = layer_index % 2 == 0
    is_first = layer_index == 0

    def exact(state_rows):
        return exact_branch(state_rows, positions, gain_vector, weight_set, head_gains, weight_out)

    branch, keys_all, values_all = exact(start_state)
    start_f = start_state.astype(jnp.float32)
    fine_state = (start_f + step_size * branch).astype(jnp.bfloat16)
    guess_term = (start_f + 2.0 * step_size * branch).astype(jnp.bfloat16)
    fine_input, received_guess = from_behind((fine_state, guess_term), "layer", 1)
    odd_branch, _, _ = exact(fine_input)
    fine_term = (fine_input.astype(jnp.float32) + step_size * odd_branch).astype(jnp.bfloat16)
    groups = ((0, row_count, token_count),)

    def coarse(state_rows):
        return coarse_branch(
            state_rows,
            positions,
            groups,
            gain_vector,
            weight_set[0],
            head_gains[0],
            keys_all,
            values_all,
            weight_out,
        )

    correction = fine_term.astype(jnp.float32) - received_guess.astype(jnp.float32)

    def advance(turn_index, carry):
        coarse_state = carry[0]
        full_step = coarse_state.astype(jnp.float32) + 2.0 * step_size * coarse(coarse_state)
        arrived = forward_hop(full_step)
        stepped = (arrived + correction).astype(jnp.bfloat16)
        passed = forward_hop(stepped.astype(jnp.float32)).astype(jnp.bfloat16)
        return (jnp.where(is_first, start_state, passed), stepped)

    coarse_state, next_state = lax.fori_loop(0, pair_count, advance, (start_state, start_state))
    pair_states = jnp.stack([coarse_state, next_state])
    settled_coarse = pair_states[0]
    settled_next = pair_states[1]
    final_branch, _, _ = exact(settled_coarse)
    relaxed = (settled_coarse.astype(jnp.float32) + step_size * final_branch).astype(jnp.bfloat16)
    corrected = jnp.where(is_even, relaxed, settled_next)
    return corrected[None]


def solution(mesh):
    in_specs = (
        P("layer", "seq", None),
        P("layer", None, None, None),
        P("layer", None, None),
        P("layer", None),
        P("layer", None, None),
    )
    out_specs = P("layer", "seq", None)
    return jax.shard_map(
        on_device, mesh=mesh, in_specs=in_specs, out_specs=out_specs, check_vma=False
    )
```

profile of v0, /device:TPU:153, one launch (start us, length us, event | category | flops | bytes accessed | tf_op | source)
XLA Modules:
  0.0 739.5 jit_solution(6677771254622350219)
XLA Ops:
  15.9 24.1 %all-gather.7.cloned.1.call-done = bf16[1024,512]{0,1:T(8,128)(2,1)} async-done(((bf16[128,512]{0,1:T(8,128)(2,1)}), bf16[1024,512]{0,1:T(8,128)(2,1)}) %all-gather.7.cloned.1.call-update) | async-done | bytes 1048592 | tf_op jit(solution)/shard_map/all_gather | solution.py:60
  44.3 24.4 %all-gather.9.cloned.1.call-done = bf16[1024,512]{1,0:T(8,128)(2,1)} async-done(((bf16[128,512]{1,0:T(8,128)(2,1)}), bf16[1024,512]{1,0:T(8,128)(2,1)}) %all-gather.9.cloned.1.call-update) | async-done | bytes 1048592 | tf_op jit(solution)/shard_map/all_gather | solution.py:61
  98.6 15.6 %all-gather.13.cloned.1.call-done = bf16[1024,512]{0,1:T(8,128)(2,1)} async-done(((bf16[128,512]{0,1:T(8,128)(2,1)}), bf16[1024,512]{0,1:T(8,128)(2,1)}) %all-gather.13.cloned.1.call-update) | async-done | bytes 1048592 | tf_op jit(solution)/shard_map/all_gather | solution.py:60
  119.2 23.6 %all-gather.11.cloned.1.call-done = bf16[1024,512]{1,0:T(8,128)(2,1)} async-done(((bf16[128,512]{1,0:T(8,128)(2,1)}), bf16[1024,512]{1,0:T(8,128)(2,1)}) %all-gather.11.cloned.1.call-update) | async-done | bytes 1048592 | tf_op jit(solution)/shard_map/all_gather | solution.py:61
  150.8 479.6 %while.13 = (s32[]{:T(128)}, bf16[128,1024]{1,0:T(8,128)(2,1)S(1)}, bf16[128,1024]{1,0:T(8,128)(2,1)}, pred[]{:T(512)}, f32[1,1024]{1,0:T(1,128)S(1)}, /*index=5...) while((s32[]{:T(128)}, bf16[128,1024]{1,0:T(8,128)(2,1)S(1)}, ...), condition=%wide.region_12.13_spmd.clone, body=%wide.region_8.12_spmd.clone.sunk | while | flops 546439424 | bytes 27688976 | solution.py:144
  159.4 14.1 %collective-permute-done = f32[128,1024]{1,0:T(8,128)S(1)} collective-permute-done((f32[128,1024]{1,0:T(8,128)S(1)}, f32[128,1024]{1,0:T(8,128)S(1)}, u32[]{:S(2)}, u32[]{:S(2)}) %collective-permute-start) | collective-permute-done | bytes 524320 | tf_op jit(solution)/shard_map/while/body/eval_jaxpr/ppermute | solution.py:13
  191.8 12.6 %collective-permute-done = f32[128,1024]{1,0:T(8,128)S(1)} collective-permute-done((f32[128,1024]{1,0:T(8,128)S(1)}, f32[128,1024]{1,0:T(8,128)S(1)}, u32[]{:S(2)}, u32[]{:S(2)}) %collective-permute-start) | collective-permute-done | bytes 524320 | tf_op jit(solution)/shard_map/while/body/eval_jaxpr/ppermute | solution.py:13
  221.2 10.5 %collective-permute-done = f32[128,1024]{1,0:T(8,128)S(1)} collective-permute-done((f32[128,1024]{1,0:T(8,128)S(1)}, f32[128,1024]{1,0:T(8,128)S(1)}, u32[]{:S(2)}, u32[]{:S(2)}) %collective-permute-start) | collective-permute-done | bytes 524320 | tf_op jit(solution)/shard_map/while/body/eval_jaxpr/ppermute | solution.py:13
  286.7 9.6 %collective-permute-done.1 = bf16[128,1024]{1,0:T(8,128)(2,1)S(1)} collective-permute-done((bf16[128,1024]{1,0:T(8,128)(2,1)S(1)}, bf16[128,1024]{1,0:T(8,128)(2,1)S(1)}, u32[]{:S(2)}, u32[]{:S(2)}) %collective-permute-start.1) | collective-permute-done | bytes 262176 | tf_op jit(solution)/shard_map/while/body/eval_jaxpr/ppermute | solution.py:13
  304.7 9.2 %collective-permute-done = f32[128,1024]{1,0:T(8,128)S(1)} collective-permute-done((f32[128,1024]{1,0:T(8,128)S(1)}, f32[128,1024]{1,0:T(8,128)S(1)}, u32[]{:S(2)}, u32[]{:S(2)}) %collective-permute-start) | collective-permute-done | bytes 524320 | tf_op jit(solution)/shard_map/while/body/eval_jaxpr/ppermute | solution.py:13
  315.9 9.4 %collective-permute-done.1 = bf16[128,1024]{1,0:T(8,128)(2,1)S(1)} collective-permute-done((bf16[128,1024]{1,0:T(8,128)(2,1)S(1)}, bf16[128,1024]{1,0:T(8,128)(2,1)S(1)}, u32[]{:S(2)}, u32[]{:S(2)}) %collective-permute-start.1) | collective-permute-done | bytes 262176 | tf_op jit(solution)/shard_map/while/body/eval_jaxpr/ppermute | solution.py:13
  333.7 9.2 %collective-permute-done = f32[128,1024]{1,0:T(8,128)S(1)} collective-permute-done((f32[128,1024]{1,0:T(8,128)S(1)}, f32[128,1024]{1,0:T(8,128)S(1)}, u32[]{:S(2)}, u32[]{:S(2)}) %collective-permute-start) | collective-permute-done | bytes 524320 | tf_op jit(solution)/shard_map/while/body/eval_jaxpr/ppermute | solution.py:13
  361.1 11.0 %collective-permute-done = f32[128,1024]{1,0:T(8,128)S(1)} collective-permute-done((f32[128,1024]{1,0:T(8,128)S(1)}, f32[128,1024]{1,0:T(8,128)S(1)}, u32[]{:S(2)}, u32[]{:S(2)}) %collective-permute-start) | collective-permute-done | bytes 524320 | tf_op jit(solution)/shard_map/while/body/eval_jaxpr/ppermute | solution.py:13
  388.9 13.0 %collective-permute-done = f32[128,1024]{1,0:T(8,128)S(1)} collective-permute-done((f32[128,1024]{1,0:T(8,128)S(1)}, f32[128,1024]{1,0:T(8,128)S(1)}, u32[]{:S(2)}, u32[]{:S(2)}) %collective-permute-start) | collective-permute-done | bytes 524320 | tf_op jit(solution)/shard_map/while/body/eval_jaxpr/ppermute | solution.py:13
  418.6 13.1 %collective-permute-done = f32[128,1024]{1,0:T(8,128)S(1)} collective-permute-done((f32[128,1024]{1,0:T(8,128)S(1)}, f32[128,1024]{1,0:T(8,128)S(1)}, u32[]{:S(2)}, u32[]{:S(2)}) %collective-permute-start) | collective-permute-done | bytes 524320 | tf_op jit(solution)/shard_map/while/body/eval_jaxpr/ppermute | solution.py:13
  449.3 12.1 %collective-permute-done = f32[128,1024]{1,0:T(8,128)S(1)} collective-permute-done((f32[128,1024]{1,0:T(8,128)S(1)}, f32[128,1024]{1,0:T(8,128)S(1)}, u32[]{:S(2)}, u32[]{:S(2)}) %collective-permute-start) | collective-permute-done | bytes 524320 | tf_op jit(solution)/shard_map/while/body/eval_jaxpr/ppermute | solution.py:13
  478.8 10.2 %collective-permute-done = f32[128,1024]{1,0:T(8,128)S(1)} collective-permute-done((f32[128,1024]{1,0:T(8,128)S(1)}, f32[128,1024]{1,0:T(8,128)S(1)}, u32[]{:S(2)}, u32[]{:S(2)}) %collective-permute-start) | collective-permute-done | bytes 524320 | tf_op jit(solution)/shard_map/while/body/eval_jaxpr/ppermute | solution.py:13
  506.4 10.5 %collective-permute-done = f32[128,1024]{1,0:T(8,128)S(1)} collective-permute-done((f32[128,1024]{1,0:T(8,128)S(1)}, f32[128,1024]{1,0:T(8,128)S(1)}, u32[]{:S(2)}, u32[]{:S(2)}) %collective-permute-start) | collective-permute-done | bytes 524320 | tf_op jit(solution)/shard_map/while/body/eval_jaxpr/ppermute | solution.py:13
  534.6 13.0 %collective-permute-done = f32[128,1024]{1,0:T(8,128)S(1)} collective-permute-done((f32[128,1024]{1,0:T(8,128)S(1)}, f32[128,1024]{1,0:T(8,128)S(1)}, u32[]{:S(2)}, u32[]{:S(2)}) %collective-permute-start) | collective-permute-done | bytes 524320 | tf_op jit(solution)/shard_map/while/body/eval_jaxpr/ppermute | solution.py:13
  566.8 15.8 %collective-permute-done = f32[128,1024]{1,0:T(8,128)S(1)} collective-permute-done((f32[128,1024]{1,0:T(8,128)S(1)}, f32[128,1024]{1,0:T(8,128)S(1)}, u32[]{:S(2)}, u32[]{:S(2)}) %collective-permute-start) | collective-permute-done | bytes 524320 | tf_op jit(solution)/shard_map/while/body/eval_jaxpr/ppermute | solution.py:13
  584.6 10.9 %collective-permute-done.1 = bf16[128,1024]{1,0:T(8,128)(2,1)S(1)} collective-permute-done((bf16[128,1024]{1,0:T(8,128)(2,1)S(1)}, bf16[128,1024]{1,0:T(8,128)(2,1)S(1)}, u32[]{:S(2)}, u32[]{:S(2)}) %collective-permute-start.1) | collective-permute-done | bytes 262176 | tf_op jit(solution)/shard_map/while/body/eval_jaxpr/ppermute | solution.py:13
  603.9 15.7 %collective-permute-done = f32[128,1024]{1,0:T(8,128)S(1)} collective-permute-done((f32[128,1024]{1,0:T(8,128)S(1)}, f32[128,1024]{1,0:T(8,128)S(1)}, u32[]{:S(2)}, u32[]{:S(2)}) %collective-permute-start) | collective-permute-done | bytes 524320 | tf_op jit(solution)/shard_map/while/body/eval_jaxpr/ppermute | solution.py:13
  635.9 62.0 %all-gather.17.cloned.1.call-done = bf16[1024,512]{0,1:T(8,128)(2,1)} async-done(((bf16[128,512]{0,1:T(8,128)(2,1)}), bf16[1024,512]{0,1:T(8,128)(2,1)}) %all-gather.17.cloned.1.call-update) | async-done | bytes 1048592 | tf_op jit(solution)/shard_map/all_gather | solution.py:60
  702.4 24.3 %all-gather.15.cloned.1.call-done = bf16[1024,512]{1,0:T(8,128)(2,1)} async-done(((bf16[128,512]{1,0:T(8,128)(2,1)}), bf16[1024,512]{1,0:T(8,128)(2,1)}) %all-gather.15.cloned.1.call-update) | async-done | bytes 1048592 | tf_op jit(solution)/shard_map/all_gather | solution.py:61
  (401 shorter events, 349.8 us)
Async XLA Ops:
  6.5 33.4 %all-gather.7.cloned.1.call-start = ((), (), s32[]{:S(2)}) async-start(), calls=%async_computation | async-start | bytes 1179648 | tf_op jit(solution)/shard_map/all_gather | solution.py:60
  12.2 56.5 %all-gather.9.cloned.1.call-start = ((), (), s32[]{:S(2)}) async-start(), calls=%async_computation.1 | async-start | bytes 1179648 | tf_op jit(solution)/shard_map/all_gather | solution.py:61
  14.5 99.6 %all-gather.13.cloned.1.call-start = ((), (), s32[]{:S(2)}) async-start(), calls=%async_computation.3 | async-start | bytes 1179648 | tf_op jit(solution)/shard_map/all_gather | solution.py:60
  87.5 55.4 %all-gather.11.cloned.1.call-start = ((), (), s32[]{:S(2)}) async-start(), calls=%async_computation.2 | async-start | bytes 1179648 | tf_op jit(solution)/shard_map/all_gather | solution.py:61
  89.8 608.2 %all-gather.17.cloned.1.call-start = ((), (), s32[]{:S(2)}) async-start(), calls=%async_computation.5 | async-start | bytes 1179648 | tf_op jit(solution)/shard_map/all_gather | solution.py:60
  95.2 53.5 %collective-permute-start.3 = (bf16[128,1024]{1,0:T(8,128)(2,1)S(1)}, bf16[128,1024]{1,0:T(8,128)(2,1)S(1)}, u32[]{:S(2)}, u32[]{:S(2)}) collective-permute-start(bf16[128,1024]{1,0:T(8,128)(2,1)S(1)} %get-tuple-element.147), channel_id=1, source_target_pairs={{0,8},{8,16},{16,24},{24,32},{32,40},{40,48},{48,56},{56,64},{64,7... | collective-permute-start | bytes 786440 | tf_op jit(solution)/shard_map/ppermute | solution.py:13
  157.2 16.4 %collective-permute-start = (f32[128,1024]{1,0:T(8,128)S(1)}, f32[128,1024]{1,0:T(8,128)S(1)}, u32[]{:S(2)}, u32[]{:S(2)}) collective-permute-start(f32[128,1024]{1,0:T(8,128)S(1)} %fusion.122), channel_id=1, source_target_pairs={{0,8},{8,16},{16,24},{24,32},{32,40},{40,48},{48,56},{56,64},{64,7... | collective-permute-start | bytes 1572872 | tf_op jit(solution)/shard_map/while/body/eval_jaxpr/ppermute | solution.py:13
  189.9 14.5 %collective-permute-start = (f32[128,1024]{1,0:T(8,128)S(1)}, f32[128,1024]{1,0:T(8,128)S(1)}, u32[]{:S(2)}, u32[]{:S(2)}) collective-permute-start(f32[128,1024]{1,0:T(8,128)S(1)} %fusion.122), channel_id=1, source_target_pairs={{0,8},{8,16},{16,24},{24,32},{32,40},{40,48},{48,56},{56,64},{64,7... | collective-permute-start | bytes 1572872 | tf_op jit(solution)/shard_map/while/body/eval_jaxpr/ppermute | solution.py:13
  219.3 12.5 %collective-permute-start = (f32[128,1024]{1,0:T(8,128)S(1)}, f32[128,1024]{1,0:T(8,128)S(1)}, u32[]{:S(2)}, u32[]{:S(2)}) collective-permute-start(f32[128,1024]{1,0:T(8,128)S(1)} %fusion.122), channel_id=1, source_target_pairs={{0,8},{8,16},{16,24},{24,32},{32,40},{40,48},{48,56},{56,64},{64,7... | collective-permute-start | bytes 1572872 | tf_op jit(solution)/shard_map/while/body/eval_jaxpr/ppermute | solution.py:13
  284.8 11.5 %collective-permute-start.1 = (bf16[128,1024]{1,0:T(8,128)(2,1)S(1)}, bf16[128,1024]{1,0:T(8,128)(2,1)S(1)}, u32[]{:S(2)}, u32[]{:S(2)}) collective-permute-start(bf16[128,1024]{1,0:T(8,128)(2,1)S(1)} %add_convert_fusion.2), channel_id=1, source_target_pairs={{0,8},{8,16},{16,24},{24,32},{32,40},{40,48},{48,56},{56,64},{64,7... | collective-permute-start | bytes 786440 | tf_op jit(solution)/shard_map/while/body/eval_jaxpr/ppermute | solution.py:13
  302.7 11.1 %collective-permute-start = (f32[128,1024]{1,0:T(8,128)S(1)}, f32[128,1024]{1,0:T(8,128)S(1)}, u32[]{:S(2)}, u32[]{:S(2)}) collective-permute-start(f32[128,1024]{1,0:T(8,128)S(1)} %fusion.122), channel_id=1, source_target_pairs={{0,8},{8,16},{16,24},{24,32},{32,40},{40,48},{48,56},{56,64},{64,7... | collective-permute-start | bytes 1572872 | tf_op jit(solution)/shard_map/while/body/eval_jaxpr/ppermute | solution.py:13
  314.0 11.3 %collective-permute-start.1 = (bf16[128,1024]{1,0:T(8,128)(2,1)S(1)}, bf16[128,1024]{1,0:T(8,128)(2,1)S(1)}, u32[]{:S(2)}, u32[]{:S(2)}) collective-permute-start(bf16[128,1024]{1,0:T(8,128)(2,1)S(1)} %add_convert_fusion.2), channel_id=1, source_target_pairs={{0,8},{8,16},{16,24},{24,32},{32,40},{40,48},{48,56},{56,64},{64,7... | collective-permute-start | bytes 786440 | tf_op jit(solution)/shard_map/while/body/eval_jaxpr/ppermute | solution.py:13
  331.7 11.1 %collective-permute-start = (f32[128,1024]{1,0:T(8,128)S(1)}, f32[128,1024]{1,0:T(8,128)S(1)}, u32[]{:S(2)}, u32[]{:S(2)}) collective-permute-start(f32[128,1024]{1,0:T(8,128)S(1)} %fusion.122), channel_id=1, source_target_pairs={{0,8},{8,16},{16,24},{24,32},{32,40},{40,48},{48,56},{56,64},{64,7... | collective-permute-start | bytes 1572872 | tf_op jit(solution)/shard_map/while/body/eval_jaxpr/ppermute | solution.py:13
  359.1 13.0 %collective-permute-start = (f32[128,1024]{1,0:T(8,128)S(1)}, f32[128,1024]{1,0:T(8,128)S(1)}, u32[]{:S(2)}, u32[]{:S(2)}) collective-permute-start(f32[128,1024]{1,0:T(8,128)S(1)} %fusion.122), channel_id=1, source_target_pairs={{0,8},{8,16},{16,24},{24,32},{32,40},{40,48},{48,56},{56,64},{64,7... | collective-permute-start | bytes 1572872 | tf_op jit(solution)/shard_map/while/body/eval_jaxpr/ppermute | solution.py:13
  386.9 14.9 %collective-permute-start = (f32[128,1024]{1,0:T(8,128)S(1)}, f32[128,1024]{1,0:T(8,128)S(1)}, u32[]{:S(2)}, u32[]{:S(2)}) collective-permute-start(f32[128,1024]{1,0:T(8,128)S(1)} %fusion.122), channel_id=1, source_target_pairs={{0,8},{8,16},{16,24},{24,32},{32,40},{40,48},{48,56},{56,64},{64,7... | collective-permute-start | bytes 1572872 | tf_op jit(solution)/shard_map/while/body/eval_jaxpr/ppermute | solution.py:13
  416.7 15.1 %collective-permute-start = (f32[128,1024]{1,0:T(8,128)S(1)}, f32[128,1024]{1,0:T(8,128)S(1)}, u32[]{:S(2)}, u32[]{:S(2)}) collective-permute-start(f32[128,1024]{1,0:T(8,128)S(1)} %fusion.122), channel_id=1, source_target_pairs={{0,8},{8,16},{16,24},{24,32},{32,40},{40,48},{48,56},{56,64},{64,7... | collective-permute-start | bytes 1572872 | tf_op jit(solution)/shard_map/while/body/eval_jaxpr/ppermute | solution.py:13
  447.4 14.0 %collective-permute-start = (f32[128,1024]{1,0:T(8,128)S(1)}, f32[128,1024]{1,0:T(8,128)S(1)}, u32[]{:S(2)}, u32[]{:S(2)}) collective-permute-start(f32[128,1024]{1,0:T(8,128)S(1)} %fusion.122), channel_id=1, source_target_pairs={{0,8},{8,16},{16,24},{24,32},{32,40},{40,48},{48,56},{56,64},{64,7... | collective-permute-start | bytes 1572872 | tf_op jit(solution)/shard_map/while/body/eval_jaxpr/ppermute | solution.py:13
  476.9 12.2 %collective-permute-start = (f32[128,1024]{1,0:T(8,128)S(1)}, f32[128,1024]{1,0:T(8,128)S(1)}, u32[]{:S(2)}, u32[]{:S(2)}) collective-permute-start(f32[128,1024]{1,0:T(8,128)S(1)} %fusion.122), channel_id=1, source_target_pairs={{0,8},{8,16},{16,24},{24,32},{32,40},{40,48},{48,56},{56,64},{64,7... | collective-permute-start | bytes 1572872 | tf_op jit(solution)/shard_map/while/body/eval_jaxpr/ppermute | solution.py:13
  504.5 12.4 %collective-permute-start = (f32[128,1024]{1,0:T(8,128)S(1)}, f32[128,1024]{1,0:T(8,128)S(1)}, u32[]{:S(2)}, u32[]{:S(2)}) collective-permute-start(f32[128,1024]{1,0:T(8,128)S(1)} %fusion.122), channel_id=1, source_target_pairs={{0,8},{8,16},{16,24},{24,32},{32,40},{40,48},{48,56},{56,64},{64,7... | collective-permute-start | bytes 1572872 | tf_op jit(solution)/shard_map/while/body/eval_jaxpr/ppermute | solution.py:13
  532.7 15.0 %collective-permute-start = (f32[128,1024]{1,0:T(8,128)S(1)}, f32[128,1024]{1,0:T(8,128)S(1)}, u32[]{:S(2)}, u32[]{:S(2)}) collective-permute-start(f32[128,1024]{1,0:T(8,128)S(1)} %fusion.122), channel_id=1, source_target_pairs={{0,8},{8,16},{16,24},{24,32},{32,40},{40,48},{48,56},{56,64},{64,7... | collective-permute-start | bytes 1572872 | tf_op jit(solution)/shard_map/while/body/eval_jaxpr/ppermute | solution.py:13
  564.9 17.7 %collective-permute-start = (f32[128,1024]{1,0:T(8,128)S(1)}, f32[128,1024]{1,0:T(8,128)S(1)}, u32[]{:S(2)}, u32[]{:S(2)}) collective-permute-start(f32[128,1024]{1,0:T(8,128)S(1)} %fusion.122), channel_id=1, source_target_pairs={{0,8},{8,16},{16,24},{24,32},{32,40},{40,48},{48,56},{56,64},{64,7... | collective-permute-start | bytes 1572872 | tf_op jit(solution)/shard_map/while/body/eval_jaxpr/ppermute | solution.py:13
  582.7 12.8 %collective-permute-start.1 = (bf16[128,1024]{1,0:T(8,128)(2,1)S(1)}, bf16[128,1024]{1,0:T(8,128)(2,1)S(1)}, u32[]{:S(2)}, u32[]{:S(2)}) collective-permute-start(bf16[128,1024]{1,0:T(8,128)(2,1)S(1)} %add_convert_fusion.2), channel_id=1, source_target_pairs={{0,8},{8,16},{16,24},{24,32},{32,40},{40,48},{48,56},{56,64},{64,7... | collective-permute-start | bytes 786440 | tf_op jit(solution)/shard_map/while/body/eval_jaxpr/ppermute | solution.py:13
  601.9 17.6 %collective-permute-start = (f32[128,1024]{1,0:T(8,128)S(1)}, f32[128,1024]{1,0:T(8,128)S(1)}, u32[]{:S(2)}, u32[]{:S(2)}) collective-permute-start(f32[128,1024]{1,0:T(8,128)S(1)} %fusion.122), channel_id=1, source_target_pairs={{0,8},{8,16},{16,24},{24,32},{32,40},{40,48},{48,56},{56,64},{64,7... | collective-permute-start | bytes 1572872 | tf_op jit(solution)/shard_map/while/body/eval_jaxpr/ppermute | solution.py:13
  633.1 93.6 %all-gather.15.cloned.1.call-start = ((), (), s32[]{:S(2)}) async-start(), calls=%async_computation.4 | async-start | bytes 1179648 | tf_op jit(solution)/shard_map/all_gather | solution.py:61
  (58 other events, 503.6 us)
Sparse Core Ops, SparseCore 0:
  12.4 27.5 all-gather.6
  41.8 26.9 all-gather.8
  87.6 26.5 all-gather.12
  115.9 26.9 all-gather.10
  633.2 64.7 all-gather.16
  699.7 26.9 all-gather.14
where the time goes:
time: 745 us; the launch traced here: 740 us
  waiting for transfers between devices  496 us (67%)
  matrix products  114 us (15%)
  starting transfers between devices  66.4 us (9%)
  local copies, waits for them, and re-layouts  37.8 us (5%)
  between operations  13.8 us (2%)
  other arithmetic  9.87 us (1%)
    ppermute x34, waiting for transfers between devices, from_behind(): return lax.ppermute(value, axis, pairs)  322 us
    all_gather x3, waiting for transfers between devices, exact_branch(): lax.all_gather(key_flat, 'seq', axis=0, tiled=True)  102 us
    all_gather x3, waiting for transfers between devices, exact_branch(): lax.all_gather(value_rows, 'seq', axis=0, tiled=True)  72.4 us
    ppermute x34, starting transfers between devices, from_behind(): return lax.ppermute(value, axis, pairs)  66.2 us
    dot_general x19, matrix products, attend(): jnp.einsum('qhe,khe->hqk', queries, keys_all, preferred_element_type=jnp....  56 us
    dot_general x19, matrix products, attend(): jnp.einsum('hqk,khe->qhe', probabilities, values_all, preferred_element_t...  30.3 us
    slice x16, local copies, waits for them, and re-layouts, coarse(): weight_set[0]  20.8 us
  transfers between devices with their start and end apart: 40, of which 39 were waited for; matrix products, arithmetic and copies ran while one was open for 5% of the time, Pallas kernels for 0%

commit v1 on v0

v1 whole, which is shorter than its diff:
```python
import functools

import jax
import jax.numpy as jnp
from jax import lax
from jax.experimental import pallas as pl
from jax.experimental.pallas import tpu as pltpu
from jax.sharding import PartitionSpec as P

EPS = 1e-06
MESH = pl.DeviceIdType.MESH
F32 = jnp.float32
BF16 = jnp.bfloat16
NT = (((1,), (1,)), ((), ()))
LOG2E = 1.4426950408889634
HEAD = 64
PACK = 4
CHUNK = 16


def dot(a, b):
    return jnp.dot(a, b, preferred_element_type=F32)


def spread_queries(q, mean_square, gain):
    rows, width = q.shape
    heads = width // HEAD
    row_head = lax.broadcasted_iota(jnp.int32, (heads, rows, width), 0)
    col_head = lax.broadcasted_iota(jnp.int32, (heads, rows, width), 2) // HEAD
    spread = jnp.where(row_head == col_head, q[None], 0.0)
    head_square = jnp.sum(spread * spread, axis=-1, keepdims=True) / HEAD
    scale = lax.rsqrt(head_square + EPS * (mean_square[None] + EPS)) * (LOG2E / 8.0)
    packed = (spread * gain).astype(BF16).reshape(heads * rows, width)
    return packed, scale.reshape(heads * rows, 1)


def mix_heads(q, mean_square, gain, kv, first_position):
    rows, width = q.shape
    tokens = kv.shape[0]
    packed, scale = spread_queries(q, mean_square, gain)
    many, wide = PACK * rows, PACK * HEAD
    outs = []
    for g in range(width // wide):
        these = slice(g * many, (g + 1) * many)
        scores = lax.dot_general(
            packed[these, g * wide:(g + 1) * wide], kv[:, g * wide:(g + 1) * wide], NT,
            preferred_element_type=F32,
        ) * scale[these]
        key_at = lax.broadcasted_iota(jnp.int32, (PACK, rows, tokens), 2).reshape(many, tokens)
        query_at = lax.broadcasted_iota(jnp.int32, (PACK, rows, tokens), 1).reshape(many, tokens)
        weights = jnp.where(key_at <= query_at + first_position, jnp.exp2(scores), 0.0)
        total = jnp.sum(weights, axis=-1, keepdims=True)
        mixed = dot(weights.astype(BF16), kv[:, width + g * wide:width + (g + 1) * wide])
        mixed = (mixed * (1.0 / total)).reshape(PACK, rows, wide)
        row_head = lax.broadcasted_iota(jnp.int32, (PACK, rows, wide), 0)
        col_head = lax.broadcasted_iota(jnp.int32, (PACK, rows, wide), 2) // HEAD
        outs.append(jnp.sum(jnp.where(row_head == col_head, mixed, 0.0), axis=0).astype(BF16))
    return jnp.concatenate(outs, axis=-1)


def kernel(layers, seqs, x_ref, wqkv, wo, gain_ref, qk_ref, out_ref,
           kv_held, kv_last, xs, base, fine_out, fine_in, term_in, cin, cout, nxt,
           ga_send, ga_recv, gb_send, gb_recv, fine_sem, term_sem, c_send, c_recv, n_send, n_recv):
    layer = lax.axis_index("layer")
    seq = lax.axis_index("seq")
    rows, width = x_ref.shape
    inner = wo.shape[0]
    chunks = rows // CHUNK
    even = lax.rem(layer, 2) == 0
    odd = jnp.logical_not(even)
    sibling = seq + 1 - 2 * lax.rem(seq, 2)

    barrier = pltpu.get_barrier_semaphore()
    for step in range(1, seqs):
        pl.semaphore_signal(barrier, inc=1, device_id={"seq": lax.rem(seq + step, seqs)}, device_id_type=MESH)
    for step in (-2, -1, 1, 2):
        other = layer + step

        @pl.when(jnp.logical_and(other >= 0, other < layers))
        def _():
            pl.semaphore_signal(barrier, inc=1, device_id={"layer": other}, device_id_type=MESH)

    near = sum(jnp.where(jnp.logical_and(layer + step >= 0, layer + step < layers), 1, 0) for step in (-2, -1, 1, 2))
    pl.semaphore_wait(barrier, seqs - 1 + near)

    def block(ref, index):
        return ref.at[pl.ds(pl.multiple_of(index * rows, rows), rows)]

    def gather_copy(kv, send, recv, slot, index, target):
        return pltpu.make_async_remote_copy(
            src_ref=block(kv, index), dst_ref=block(kv, index), send_sem=send.at[slot], recv_sem=recv.at[index],
            device_id={"seq": target}, device_id_type=MESH)

    def exact(kv, send, recv):
        x = xs[...]
        mean_square = jnp.mean(x * x, axis=-1, keepdims=True)
        y = (x * gain_ref[...]).astype(BF16)
        k = dot(y, wqkv[1])
        same = lax.broadcasted_iota(jnp.int32, (inner, inner), 0) // HEAD
        same = same == lax.broadcasted_iota(jnp.int32, (inner, inner), 1) // HEAD
        head_square = dot((k * k).astype(BF16), same.astype(BF16)) / HEAD
        k = k * lax.rsqrt(head_square + EPS * (mean_square + EPS)) * qk_ref[1:2, :]
        here = pl.ds(pl.multiple_of(seq * rows, rows), rows)
        kv[here, 0:inner] = k.astype(BF16)
        kv[here, inner:2 * inner] = (dot(y, wqkv[2]) * lax.rsqrt(mean_square + EPS)).astype(BF16)
        copies = []
        for i in range(1, seqs // 2):
            copies.append(gather_copy(kv, send, recv, i, seq, lax.rem(seq + 2 * i, seqs)))
        copies.append(gather_copy(kv, send, recv, 0, seq, sibling))
        for copy in copies:
            copy.start()
        q = dot(y, wqkv[0])
        for i in range(1, seqs // 2):
            source = lax.rem(seq + 2 * i, seqs)
            copy = gather_copy(kv, send, recv, seqs // 2 + i, source, sibling)
            copy.wait_recv()
            copy.start()
            copies.append(copy)
        gather_copy(kv, send, recv, 0, sibling, sibling).wait_recv()
        for i in range(1, seqs // 2):
            gather_copy(kv, send, recv, 0, lax.rem(sibling + 2 * i, seqs), sibling).wait_recv()
        for copy in copies:
            copy.wait_send()
        mix = mix_heads(q, mean_square, qk_ref[0:1, :], kv, seq * rows)
        return x, dot(mix, wo[...])

    def whole(src, dst, sems, target):
        return pltpu.make_async_remote_copy(
            src_ref=src, dst_ref=dst, send_sem=sems.at[0], recv_sem=sems.at[1],
            device_id={"layer": target}, device_id_type=MESH)

    def piece(src, dst, send, recv, c, target):
        at = pl.ds(pl.multiple_of(c * CHUNK, CHUNK), CHUNK)
        return pltpu.make_async_remote_copy(
            src_ref=src.at[at], dst_ref=dst.at[at], send_sem=send.at[c], recv_sem=recv.at[c],
            device_id={"layer": target}, device_id_type=MESH)

    def each_chunk(body):
        def step(c, carry):
            body(c)
            return carry
        lax.fori_loop(0, chunks, step, 0)

    @pl.when(even)
    def _():
        xs[...] = x_ref[...].astype(F32)

    @pl.when(odd)
    def _():
        whole(fine_out, fine_in, fine_sem, layer - 1).wait_recv()
        xs[...] = fine_in[...].astype(F32)

    x, branch = exact(kv_held, ga_send, ga_recv)
    fine_out[...] = (x + branch).astype(BF16)
    base[...] = -(x + 2.0 * branch)

    @pl.when(even)
    def _():
        copy = whole(fine_out, fine_in, fine_sem, layer + 1)
        copy.start()
        copy.wait_send()

    @pl.when(layer <= 1)
    def _():
        out_ref[...] = fine_out[...]

    @pl.when(layer == 1)
    def _():
        each_chunk(lambda c: piece(fine_out, cin, c_send, c_recv, c, layer + 1).start())
        each_chunk(lambda c: piece(fine_out, cin, c_send, c_recv, c, layer + 1).wait_send())

    @pl.when(jnp.logical_and(odd, layer > 1))
    def _():
        copy = whole(fine_out, term_in, term_sem, layer - 1)
        copy.start()
        copy.wait_send()

    @pl.when(jnp.logical_and(even, layer > 0))
    def _():
        whole(fine_out, term_in, term_sem, layer + 1).wait_recv()
        base[...] = base[...] + term_in[...].astype(F32)

        def advance(c):
            piece(cout, cin, c_send, c_recv, c, layer - 1).wait_recv()
            at = pl.ds(pl.multiple_of(c * CHUNK, CHUNK), CHUNK)
            x = cin[at, :].astype(F32)
            xs[at, :] = x
            mean_square = jnp.mean(x * x, axis=-1, keepdims=True)
            q = dot((x * gain_ref[...]).astype(BF16), wqkv[0])
            mix = mix_heads(q, mean_square, qk_ref[0:1, :], kv_held, seq * rows + c * CHUNK)
            cout[at, :] = (x + 2.0 * dot(mix, wo[...]) + base[at, :]).astype(BF16)

            @pl.when(layer < layers - 2)
            def _():
                piece(cout, cin, c_send, c_recv, c, layer + 2).start()

            piece(cout, nxt, n_send, n_recv, c, layer + 1).start()

        each_chunk(advance)
        x, branch = exact(kv_last, gb_send, gb_recv)
        out_ref[...] = (x + branch).astype(BF16)

        @pl.when(layer < layers - 2)
        def _():
            each_chunk(lambda c: piece(cout, cin, c_send, c_recv, c, layer + 2).wait_send())

        each_chunk(lambda c: piece(cout, nxt, n_send, n_recv, c, layer + 1).wait_send())

    @pl.when(jnp.logical_and(odd, layer > 1))
    def _():
        each_chunk(lambda c: piece(cout, nxt, n_send, n_recv, c, layer - 1).wait_recv())
        out_ref[...] = nxt[...]


def solution(mesh):
    layers, seqs = mesh.shape["layer"], mesh.shape["seq"]

    def on_device(states, w_qkv, w_out, norm_gain, qk_gain):
        rows, width = states.shape[1:]
        inner = w_out.shape[1]
        gains = jnp.tile(qk_gain[0], (1, inner // HEAD))
        vmem = pl.BlockSpec(memory_space=pltpu.VMEM)
        dma = pltpu.SemaphoreType.DMA
        state = pltpu.VMEM((rows, width), BF16)
        wide = pltpu.VMEM((rows, width), F32)
        gathered = pltpu.VMEM((rows * seqs, 2 * inner), BF16)
        out = pl.pallas_call(
            functools.partial(kernel, layers, seqs),
            out_shape=jax.ShapeDtypeStruct((rows, width), BF16),
            in_specs=[vmem] * 5,
            out_specs=vmem,
            scratch_shapes=[
                gathered, gathered, wide, wide, state, state, state, state, state, state,
                dma((seqs,)), dma((seqs,)), dma((seqs,)), dma((seqs,)), dma((2,)), dma((2,)),
                dma((rows // CHUNK,)), dma((rows // CHUNK,)), dma((rows // CHUNK,)), dma((rows // CHUNK,)),
            ],
            compiler_params=pltpu.CompilerParams(
                collective_id=0, has_side_effects=True, vmem_limit_bytes=56 << 20),
        )(states[0], w_qkv[0], w_out[0], norm_gain, gains)
        return out[None]

    in_specs = (
        P("layer", "seq", None),
        P("layer", None, None, None),
        P("layer", None, None),
        P("layer", None),
        P("layer", None, None),
    )
    return jax.shard_map(
        on_device, mesh=mesh, in_specs=in_specs, out_specs=P("layer", "seq", None), check_vma=False
    )
```

time: 745 us -> 155 us (0.21)
  the two profiles are of different devices: /device:TPU:153 before, /device:TPU:217 now
where the time goes in v1:
time: 155 us; the launch traced here: 154 us
  Pallas kernels  151 us (97%)
  local copies, waits for them, and re-layouts  3.02 us (2%)
    pallas_call x1, Pallas kernels, on_device(): pl.pallas_call(functools.partial(kernel, layers, seqs), out_shape=jax.Sha...  151 us

profile of v1, /device:TPU:217, one launch (start us, length us, event | category | flops | bytes accessed | tf_op | source)
XLA Modules:
  0.0 154.5 jit_solution(7851330795860515810)
XLA Ops:
  0.0 0.7 tile.11
  0.7 0.7 tile.12.qk_ref
  1.4 151.4 %shard_map.55 = bf16[128,1024]{1,0:T(8,128)(2,1)} custom-call(bf16[128,1024]{1,0:T(8,128)(2,1)} %bitcast.8, bf16[3,1024,512]{2,1,0:T(8,128)(2,1)} %bitcast.5, bf16[512,1024]{1,0:T(8,128)(2,1)} %bitcast.7, f32[1,1024]{1,0:T(1,128)} %gain_ref.1, f32[2,512]{1,0:T(2,128)} %tile.12.qk_ref), custom_call_target="tpu_custom_call" | custom-call | tf_op jit(solution)/shard_map/pallas_call | solution.py:227
  152.8 1.7 %copy.7 = bf16[1,128,1024]{2,1,0:T(8,128)(2,1)} copy(bf16[1,128,1024]{2,1,0:T(8,128)(2,1)} %bitcast.6) | data formatting | bytes 524288

commit v2 on v1

v2 whole, which is shorter than its diff:
```python
import functools

import jax
import jax.numpy as jnp
from jax import lax
from jax.experimental import pallas as pl
from jax.experimental.pallas import tpu as pltpu
from jax.sharding import PartitionSpec as P

EPS = 1e-06
MESH = pl.DeviceIdType.MESH
F32 = jnp.float32
BF16 = jnp.bfloat16
NT = (((1,), (1,)), ((), ()))
LOG2E = 1.4426950408889634
HEAD = 64
PACK = 4
MEMBERS = 4
GROUP = 2 * MEMBERS
QUARTERS = 4


def dot(a, b):
    return jnp.dot(a, b, preferred_element_type=F32)


def spread_queries(q, mean_square, gain):
    rows, width = q.shape
    heads = width // HEAD
    row_head = lax.broadcasted_iota(jnp.int32, (heads, rows, width), 0)
    col_head = lax.broadcasted_iota(jnp.int32, (heads, rows, width), 2) // HEAD
    spread = jnp.where(row_head == col_head, q[None], 0.0)
    head_square = jnp.sum(spread * spread, axis=-1, keepdims=True) / HEAD
    scale = lax.rsqrt(head_square + EPS * (mean_square[None] + EPS)) * (LOG2E / 8.0)
    packed = (spread * gain).astype(BF16).reshape(heads * rows, width)
    return packed, scale.reshape(heads * rows, 1)


def mix_heads(q, mean_square, gain, columns, first_position):
    rows, width = q.shape
    packed, scale = spread_queries(q, mean_square, gain)
    many, wide = PACK * rows, PACK * HEAD
    outs = []
    for g in range(width // wide):
        these = slice(g * many, (g + 1) * many)
        keys = columns(g * wide, wide)
        tokens = keys.shape[0]
        scores = lax.dot_general(
            packed[these, g * wide:(g + 1) * wide], keys, NT, preferred_element_type=F32
        ) * scale[these]
        key_at = lax.broadcasted_iota(jnp.int32, (PACK, rows, tokens), 2).reshape(many, tokens)
        query_at = lax.broadcasted_iota(jnp.int32, (PACK, rows, tokens), 1).reshape(many, tokens)
        weights = jnp.where(key_at <= query_at + first_position, jnp.exp2(scores), 0.0)
        total = jnp.sum(weights, axis=-1, keepdims=True)
        mixed = dot(weights.astype(BF16), columns(width + g * wide, wide))
        mixed = (mixed * (1.0 / total)).reshape(PACK, rows, wide)
        row_head = lax.broadcasted_iota(jnp.int32, (PACK, rows, wide), 0)
        col_head = lax.broadcasted_iota(jnp.int32, (PACK, rows, wide), 2) // HEAD
        outs.append(jnp.sum(jnp.where(row_head == col_head, mixed, 0.0), axis=0).astype(BF16))
    return jnp.concatenate(outs, axis=-1)


def kernel(layers, seqs, x_hbm, wqkv_hbm, wo_hbm, gain_hbm, qk_hbm, out_ref,
           wq_all, wo_all, kv_all, kv_last, wkv, x_in, fine_in, cin, nxt, fine_out, guess_out,
           guess_all, term_all, chain, gains_all, qk_raw, gain_raw, xs, ys,
           load, gather_send, gather_recv, spread_send, spread_recv,
           fine_send, fine_recv, guess_send, guess_recv, term_send, term_recv,
           cin_send, cin_recv, nxt_send, nxt_recv, hop_sem, gain_send, gain_recv):
    layer = lax.axis_index("layer")
    seq = lax.axis_index("seq")
    units, unit, width = x_in.shape
    inner = width // 2
    group = layer // GROUP
    inside = lax.rem(layer, GROUP)
    member = inside // 2
    core = lax.rem(seq, 2)
    side = lax.rem(seq // 2, 2)
    even = lax.rem(layer, 2) == 0
    odd = jnp.logical_not(even)
    sibling = seq + 1 - 2 * core
    right, left = lax.rem(seq + 2, seqs), lax.rem(seq + seqs - 2, seqs)
    across = lax.rem(seq + 4, seqs)
    groups = layers // GROUP

    barrier = pltpu.get_barrier_semaphore()
    for other in (sibling, right, left):
        pl.semaphore_signal(barrier, inc=1, device_id={"seq": other}, device_id_type=MESH)
    for step in range(1, GROUP):
        other = group * GROUP + lax.rem(inside + step, GROUP)
        pl.semaphore_signal(barrier, inc=1, device_id={"layer": other}, device_id_type=MESH)

    @pl.when(group > 0)
    def _():
        pl.semaphore_signal(barrier, inc=1, device_id={"layer": layer - GROUP}, device_id_type=MESH)

    @pl.when(group < groups - 1)
    def _():
        pl.semaphore_signal(barrier, inc=1, device_id={"layer": layer + GROUP}, device_id_type=MESH)

    greeted = 3 + GROUP - 1 + jnp.where(group > 0, 1, 0) + jnp.where(group < groups - 1, 1, 0)

    loads = [
        pltpu.make_async_copy(x_hbm, x_in, load.at[0]),
        pltpu.make_async_copy(gain_hbm, gain_raw, load.at[1]),
        pltpu.make_async_copy(qk_hbm, qk_raw, load.at[2]),
        pltpu.make_async_copy(wqkv_hbm.at[1], wkv.at[0], load.at[3]),
        pltpu.make_async_copy(wqkv_hbm.at[2], wkv.at[1], load.at[4]),
        pltpu.make_async_copy(wqkv_hbm.at[0], wq_all.at[member], load.at[5]),
        pltpu.make_async_copy(wo_hbm, wo_all.at[member], load.at[6]),
    ]
    for copy in loads:
        copy.start()
    for copy in loads[:3]:
        copy.wait()
    gains_all[member, 0:1, :] = gain_raw[...]
    gains_all[member, 1:2, :] = jnp.concatenate([qk_raw[0:1, :]] * (inner // HEAD) + [qk_raw[1:2, :]] * (inner // HEAD), axis=-1)
    for copy in loads[3:]:
        copy.wait()
    norm_gain = gains_all[member, 0:1, :]
    query_gain = gains_all[member, 1:2, 0:inner]
    key_gain = gains_all[member, 1:2, inner:width]

    def remote(src, dst, send, recv, **target):
        return pltpu.make_async_remote_copy(
            src_ref=src, dst_ref=dst, send_sem=send, recv_sem=recv, device_id=target, device_id_type=MESH)

    def member_layer(m):
        return group * GROUP + 2 * m

    mine, others = 2 * side + core, 2 * (1 - side) + core
    sent = []

    def part(m, quarter, p):
        if p == 0:
            return wq_all.at[m, quarter]
        if p == 1:
            return wo_all.at[m, quarter]
        return kv_all.at[m, 2 * quarter + p - 2]

    def spread_copy(slot, m, quarter, p, **target):
        ref = part(m, quarter, p)
        return remote(ref, ref, spread_send.at[slot], spread_recv.at[m, quarter, p], **target)

    def hand(m, quarter, p, **target):
        copy = spread_copy(len(sent), m, quarter, p, **target)
        copy.start()
        sent.append(copy)

    def await_part(m, quarter, p):
        spread_copy(0, m, quarter, p, seq=sibling).wait_recv()

    def nth(step):
        return lax.rem(member + step + MEMBERS, MEMBERS)

    def spread_first(parts):
        for p in parts:
            hand(member, mine, p, layer=member_layer(nth(1)))
            hand(member, mine, p, layer=member_layer(nth(-1)))

    def spread_near(parts):
        for p in parts:
            for step in (-1, 1):
                m = nth(step)
                await_part(m, mine, p)
                if step == -1 and p % 2 == 0:
                    hand(m, mine, p, layer=member_layer(nth(1)))
                if step == 1 and p % 2 == 1:
                    hand(m, mine, p, layer=member_layer(nth(-1)))
                hand(m, mine, p, seq=right if p % 2 == 0 else left)
                hand(m, mine, p, seq=sibling)

    def spread_far(parts):
        for p in parts:
            m = nth(2)
            await_part(m, mine, p)
            hand(m, mine, p, seq=right if p % 2 == 0 else left)
            hand(m, mine, p, seq=sibling)

    def spread_side(parts, steps):
        for step in steps:
            for p in parts:
                m = nth(step)
                await_part(m, others, p)
                hand(m, others, p, seq=sibling)

    def exact(source, ready, kv, send, recv, between):
        copies = []

        def at(block, u):
            return kv(block).at[pl.ds(u * unit, unit)]

        def push(block, u, target):
            copy = remote(at(block, u), at(block, u), send.at[len(copies)], recv.at[block, u], seq=target)
            copy.start()
            copies.append(copy)

        def arrived(block, u):
            remote(at(block, u), at(block, u), send.at[0], recv.at[block, u], seq=sibling).wait_recv()

        same = lax.broadcasted_iota(jnp.int32, (inner, inner), 0) // HEAD
        same = (same == lax.broadcasted_iota(jnp.int32, (inner, inner), 1) // HEAD).astype(BF16)
        for u in range(units):
            ready(u)
            here = pl.ds(u * unit, unit)
            x = source[u].astype(F32)
            xs[here, :] = x
            mean_square = jnp.mean(x * x, axis=-1, keepdims=True)
            y = (x * norm_gain).astype(BF16)
            ys[here, :] = y
            k = dot(y, wkv[0].reshape(width, inner))
            head_square = dot((k * k).astype(BF16), same) / HEAD
            k = k * lax.rsqrt(head_square + EPS * (mean_square + EPS)) * key_gain
            at(seq, u)[:, 0:inner] = k.astype(BF16)
            at(seq, u)[:, inner:width] = (dot(y, wkv[1].reshape(width, inner)) * lax.rsqrt(mean_square + EPS)).astype(BF16)
            if u == 0:
                between()
            push(seq, u, right)
            push(seq, u, left)
            push(seq, u, sibling)
        for u in range(units):
            arrived(left, u)
            if u % 2 == 0:
                push(left, u, right)
            push(left, u, sibling)
            arrived(right, u)
            if u % 2 == 1:
                push(right, u, left)
            push(right, u, sibling)
        for u in range(units):
            arrived(across, u)
            push(across, u, sibling)
        for step in (0, 2, 6, 4):
            for u in range(units):
                arrived(lax.rem(sibling + step, seqs), u)
        x = xs[...]
        mean_square = jnp.mean(x * x, axis=-1, keepdims=True)
        q = dot(ys[...], wq_all[member].reshape(width, inner))

        def columns(start, size):
            return kv(slice(None))[:, :, start:start + size].reshape(seqs * units * unit, size)

        mix = mix_heads(q, mean_square, query_gain, columns, seq * units * unit)
        branch = dot(mix, wo_all[member].reshape(inner, width))
        return x, branch, copies

    def held(block):
        return kv_all.at[member, block]

    def last(block):
        return kv_last.at[block]

    def fine_copy(u, target):
        return remote(fine_out.at[u], fine_in.at[u], fine_send.at[u], fine_recv.at[u], layer=target)

    @pl.when(even)
    def _():
        for u in range(units):
            fine_in[u] = x_in[u]

    def fine_ready(u):
        @pl.when(odd)
        def _():
            if u == 0:
                pl.semaphore_wait(barrier, greeted)
            fine_copy(u, layer - 1).wait_recv()

    def meet():
        @pl.when(even)
        def _():
            pl.semaphore_wait(barrier, greeted)

    def gain_copy(step):
        ref = gains_all.at[member]
        return remote(ref, ref, gain_send.at[step - 1], gain_recv.at[member], layer=member_layer(nth(step)))

    x, branch, copies = exact(fine_in, fine_ready, held, gather_send.at[0], gather_recv.at[0], meet)
    fine_out[...] = (x + branch).astype(BF16).reshape(units, unit, width)

    def guess_copy(u, m):
        return remote(guess_out.at[u], guess_all.at[m], guess_send.at[u], guess_recv.at[m], layer=member_layer(u))

    def term_copy(u):
        return remote(fine_out.at[u], term_all.at[member], term_send.at[u], term_recv.at[member], layer=member_layer(u))

    def start_copy(u):
        return remote(fine_out.at[u], chain.at[0], term_send.at[u], hop_sem.at[1], layer=member_layer(u))

    @pl.when(odd)
    def _():
        @pl.when(layer == 1)
        def _():
            for u in range(units):
                start_copy(u).start()
            out_ref[...] = fine_out[...]

        @pl.when(layer > 1)
        def _():
            for u in range(units):
                term_copy(u).start()

        for copy in copies:
            copy.wait_send()
        for u in range(units):
            term_copy(u).wait_send()

        @pl.when(layer > 1)
        def _():
            for u in range(units):
                remote(chain.at[0], nxt.at[u], nxt_send.at[0], nxt_recv.at[u], layer=layer - 1).wait_recv()
            out_ref[...] = nxt[...]

    @pl.when(even)
    def _():
        for u in range(units):
            fine_copy(u, layer + 1).start()
        guess_out[...] = (x + 2.0 * branch).astype(BF16).reshape(units, unit, width)
        for u in range(units):
            @pl.when(jnp.logical_and(u != member, layer > 0))
            def _():
                guess_copy(u, member).start()
        guess_all[member] = guess_out[member]
        for step in (1, 2, 3):
            gain_copy(step).start()
        spread_first((0, 1))
        spread_first((2, 3))
        spread_near((0, 1))
        spread_far((0, 1))
        spread_near((2, 3))
        spread_side((0, 1), (-1, 1, 2))
        spread_far((2, 3))
        spread_side((2, 3), (-1, 1, 2))
        for step in (1, 2, 3):
            m = nth(step)
            for p in range(4):
                await_part(m, 2 * side + 1 - core, p)
                await_part(m, 2 * (1 - side) + 1 - core, p)
            remote(gains_all.at[m], gains_all.at[m], gain_send.at[0], gain_recv.at[m], seq=sibling).wait_recv()

        def cin_copy(m):
            return remote(chain.at[m], cin.at[member], cin_send.at[m], cin_recv.at[member], layer=member_layer(m))

        def nxt_copy(m):
            return remote(chain.at[m + 1], nxt.at[member], nxt_send.at[m], nxt_recv.at[member], layer=member_layer(m) + 1)

        def hop_copy(target):
            return remote(chain.at[MEMBERS], chain.at[0], hop_sem.at[0], hop_sem.at[1], layer=target)

        hop_copy(lax.rem(layer + GROUP, layers)).wait_recv()

        def advance(m, carry):
            first = jnp.logical_and(group == 0, m == 0)

            @pl.when(first)
            def _():
                chain[m + 1] = chain[m]

            @pl.when(jnp.logical_not(first))
            def _():
                @pl.when(m != member)
                def _():
                    cin_copy(m).start()
                    remote(guess_out.at[0], guess_all.at[m], guess_send.at[0], guess_recv.at[m], layer=layer + 1).wait_recv()

                @pl.when(m == member)
                def _():
                    cin[member] = chain[m]

                remote(fine_out.at[0], term_all.at[m], term_send.at[0], term_recv.at[m], layer=layer + 1).wait_recv()
                x = chain[m].astype(F32)
                mean_square = jnp.mean(x * x, axis=-1, keepdims=True)
                q = dot((x * gains_all[m, 0:1, :]).astype(BF16), wq_all[m].reshape(width, inner))

                def columns(start, size):
                    return kv_all[m, :, :, start:start + size].reshape(seqs * units * unit, size)

                mix = mix_heads(q, mean_square, gains_all[m, 1:2, 0:inner], columns, (seq * units + member) * unit)
                branch = dot(mix, wo_all[m].reshape(inner, width))
                correction = term_all[m].astype(F32) - guess_all[m].astype(F32)
                chain[m + 1] = (x + 2.0 * branch + correction).astype(BF16)
                nxt_copy(m).start()

            return carry

        lax.fori_loop(0, MEMBERS, advance, 0)

        @pl.when(group < groups - 1)
        def _():
            hop_copy(layer + GROUP).start()

        def cin_ready(u):
            @pl.when(u != member)
            def _():
                remote(chain.at[0], cin.at[u], cin_send.at[0], cin_recv.at[u], layer=layer + 1).wait_recv()

        @pl.when(layer == 0)
        def _():
            out_ref[...] = fine_out[...]

        @pl.when(layer > 0)
        def _():
            x, branch, more = exact(cin, cin_ready, last, gather_send.at[1], gather_recv.at[1], lambda: None)
            out_ref[...] = (x + branch).astype(BF16).reshape(units, unit, width)
            for copy in more:
                copy.wait_send()

        for copy in copies:
            copy.wait_send()
        for copy in sent:
            copy.wait_send()
        for step in (1, 2, 3):
            gain_copy(step).wait_send()
        for u in range(units):
            fine_copy(u, layer + 1).wait_send()

            @pl.when(jnp.logical_and(u != member, layer > 0))
            def _():
                guess_copy(u, member).wait_send()

        def drain(m, carry):
            @pl.when(jnp.logical_not(jnp.logical_and(group == 0, m == 0)))
            def _():
                nxt_copy(m).wait_send()

                @pl.when(m != member)
                def _():
                    cin_copy(m).wait_send()

            return carry

        lax.fori_loop(0, MEMBERS, drain, 0)

        @pl.when(group < groups - 1)
        def _():
            hop_copy(layer + GROUP).wait_send()


def solution(mesh):
    layers, seqs = mesh.shape["layer"], mesh.shape["seq"]

    def on_device(states, w_qkv, w_out, norm_gain, qk_gain):
        rows, width = states.shape[1:]
        inner = w_out.shape[1]
        unit = rows // MEMBERS
        hbm = pl.BlockSpec(memory_space=pl.ANY)
        dma = pltpu.SemaphoreType.DMA
        state = pltpu.VMEM((MEMBERS, unit, width), BF16)
        out = pl.pallas_call(
            functools.partial(kernel, layers, seqs),
            out_shape=jax.ShapeDtypeStruct((MEMBERS, unit, width), BF16),
            in_specs=[hbm] * 5,
            out_specs=pl.BlockSpec(memory_space=pltpu.VMEM),
            scratch_shapes=[
                pltpu.VMEM((MEMBERS, QUARTERS, width // QUARTERS, inner), BF16),
                pltpu.VMEM((MEMBERS, QUARTERS, inner // QUARTERS, width), BF16),
                pltpu.VMEM((MEMBERS, seqs, rows, 2 * inner), BF16),
                pltpu.VMEM((seqs, rows, 2 * inner), BF16),
                pltpu.VMEM((2, QUARTERS, width // QUARTERS, inner), BF16),
                state, state, state, state, state, state, state, state,
                pltpu.VMEM((MEMBERS + 1, unit, width), BF16),
                pltpu.VMEM((MEMBERS, 8, width), F32),
                pltpu.VMEM((2, HEAD), F32),
                pltpu.VMEM((1, width), F32),
                pltpu.VMEM((rows, width), F32),
                pltpu.VMEM((rows, width), BF16),
                dma((7,)), dma((2, 28)), dma((2, seqs, MEMBERS)), dma((48,)), dma((MEMBERS, QUARTERS, 4)),
                dma((4,)), dma((4,)), dma((4,)), dma((4,)), dma((4,)), dma((4,)),
                dma((4,)), dma((4,)), dma((4,)), dma((4,)), dma((2,)), dma((3,)), dma((4,)),
            ],
            compiler_params=pltpu.CompilerParams(
                collective_id=0, has_side_effects=True, vmem_limit_bytes=56 << 20),
        )(
            states.reshape(MEMBERS, unit, width),
            w_qkv.reshape(3, QUARTERS, width // QUARTERS, inner),
            w_out.reshape(QUARTERS, inner // QUARTERS, width),
            norm_gain, qk_gain[0],
        )
        return out.reshape(1, rows, width)

    in_specs = (
        P("layer", "seq", None),
        P("layer", None, None, None),
        P("layer", None, None),
        P("layer", None),
        P("layer", None, None),
    )
    return jax.shard_map(
        on_device, mesh=mesh, in_specs=in_specs, out_specs=P("layer", "seq", None), check_vma=False
    )
```

time: 155 us -> 144 us (0.929)
  the two profiles are of different devices: /device:TPU:217 before, /device:TPU:153 now
where the time goes in v2:
time: 144 us
  Pallas kernels  142 us (99%)
  local copies, waits for them, and re-layouts  1.67 us (1%)
    pallas_call x1, Pallas kernels, on_device(): pl.pallas_call(functools.partial(kernel, layers, seqs), out_shape=jax.Sha...  142 us

profile of v2, /device:TPU:153, one launch (start us, length us, event | category | flops | bytes accessed | tf_op | source)
XLA Modules:
  0.0 144.0 jit_solution(1882402111003691404)
XLA Ops:
  0.0 142.3 %shard_map.55 = bf16[4,32,1024]{2,1,0:T(8,128)(2,1)} custom-call(bf16[4,32,1024]{2,1,0:T(8,128)(2,1)} %bitcast.8, bf16[3,4,256,512]{3,2,1,0:T(8,128)(2,1)} %bitcast.5, bf16[4,128,1024]{2,1,0:T(8,128)(2,1)} %bitcast.7, f32[1,1024]{1,0:T(1,128)} %gain_hbm.1, f32[2,64]{1,0:T(2,128)} %bitcast.9), custom_call_target="tpu_custom_call" | custom-call | tf_op jit(solution)/shard_map/pallas_call | solution.py:447
  142.3 1.7 %copy.7 = bf16[1,128,1024]{2,1,0:T(8,128)(2,1)} copy(bf16[1,128,1024]{2,1,0:T(8,128)(2,1)} %bitcast.6) | data formatting | bytes 524288

commit v3 on v2

--- a/solution.py
+++ b/solution.py
@@ -142,9 +142,8 @@
         return remote(ref, ref, spread_send.at[slot], spread_recv.at[m, quarter, p], **target)
 
     def hand(m, quarter, p, **target):
-        copy = spread_copy(len(sent), m, quarter, p, **target)
-        copy.start()
-        sent.append(copy)
+        spread_copy(len(sent), m, quarter, p, **target).start()
+        sent.append(p)
 
     def await_part(m, quarter, p):
         spread_copy(0, m, quarter, p, seq=sibling).wait_recv()
@@ -152,38 +151,30 @@
     def nth(step):
         return lax.rem(member + step + MEMBERS, MEMBERS)
 
-    def spread_first(parts):
+    def spread_first(step, parts):
         for p in parts:
-            hand(member, mine, p, layer=member_layer(nth(1)))
-            hand(member, mine, p, layer=member_layer(nth(-1)))
-
-    def spread_near(parts):
-        for p in parts:
-            for step in (-1, 1):
-                m = nth(step)
-                await_part(m, mine, p)
-                if step == -1 and p % 2 == 0:
-                    hand(m, mine, p, layer=member_layer(nth(1)))
-                if step == 1 and p % 2 == 1:
-                    hand(m, mine, p, layer=member_layer(nth(-1)))
-                hand(m, mine, p, seq=right if p % 2 == 0 else left)
-                hand(m, mine, p, seq=sibling)
-
-    def spread_far(parts):
-        for p in parts:
-            m = nth(2)
-            await_part(m, mine, p)
-            hand(m, mine, p, seq=right if p % 2 == 0 else left)
-            hand(m, mine, p, seq=sibling)
-
-    def spread_side(parts, steps):
-        for step in steps:
-            for p in parts:
-                m = nth(step)
-                await_part(m, others, p)
-                hand(m, others, p, seq=sibling)
-
-    def exact(source, ready, kv, send, recv, between):
+            hand(member, mine, p, layer=member_layer(nth(step)))
+
+    def spread_near(step, p):
+        m = nth(step)
+        await_part(m, mine, p)
+        if (step == -1) == (p % 2 == 0):
+            hand(m, mine, p, layer=member_layer(nth(-step)))
+        hand(m, mine, p, seq=right if p % 2 == 0 else left)
+        hand(m, mine, p, seq=sibling)
+
+    def spread_far(p):
+        m = nth(2)
+        await_part(m, mine, p)
+        hand(m, mine, p, seq=right if p % 2 == 0 else left)
+        hand(m, mine, p, seq=sibling)
+
+    def spread_side(step, p):
+        m = nth(step)
+        await_part(m, others, p)
+        hand(m, others, p, seq=sibling)
+
+    def exact(source, ready, kv, send, recv, meet, pushed, gathered):
         copies = []
 
         def at(block, u):
@@ -213,10 +204,11 @@
             at(seq, u)[:, 0:inner] = k.astype(BF16)
             at(seq, u)[:, inner:width] = (dot(y, wkv[1].reshape(width, inner)) * lax.rsqrt(mean_square + EPS)).astype(BF16)
             if u == 0:
-                between()
+                meet()
             push(seq, u, right)
             push(seq, u, left)
             push(seq, u, sibling)
+        pushed()
         for u in range(units):
             arrived(left, u)
             if u % 2 == 0:
@@ -232,6 +224,7 @@
         for step in (0, 2, 6, 4):
             for u in range(units):
                 arrived(lax.rem(sibling + step, seqs), u)
+        gathered()
         x = xs[...]
         mean_square = jnp.mean(x * x, axis=-1, keepdims=True)
         q = dot(ys[...], wq_all[member].reshape(width, inner))
@@ -269,11 +262,29 @@
         def _():
             pl.semaphore_wait(barrier, greeted)
 
+    def pushed():
+        @pl.when(even)
+        def _():
+            spread_first(1, (0, 1))
+            spread_first(-1, (1, 0))
+            for step in (1, 2, 3):
+                gain_copy(step).start()
+
+    def gathered():
+        @pl.when(even)
+        def _():
+            spread_first(-1, (3, 2))
+            spread_near(-1, 0)
+            spread_near(1, 1)
+
+    def nothing():
+        pass
+
     def gain_copy(step):
         ref = gains_all.at[member]
         return remote(ref, ref, gain_send.at[step - 1], gain_recv.at[member], layer=member_layer(nth(step)))
 
-    x, branch, copies = exact(fine_in, fine_ready, held, gather_send.at[0], gather_recv.at[0], meet)
+    x, branch, copies = exact(fine_in, fine_ready, held, gather_send.at[0], gather_recv.at[0], meet, pushed, gathered)
     fine_out[...] = (x + branch).astype(BF16).reshape(units, unit, width)
 
     def guess_copy(u, m):
@@ -313,22 +324,37 @@
     def _():
         for u in range(units):
             fine_copy(u, layer + 1).start()
+        spread_near(-1, 1)
+        spread_near(1, 0)
         guess_out[...] = (x + 2.0 * branch).astype(BF16).reshape(units, unit, width)
+        for u in range(units):
+            fine_copy(u, layer + 1).wait_send()
+        spread_first(1, (2, 3))
         for u in range(units):
             @pl.when(jnp.logical_and(u != member, layer > 0))
             def _():
                 guess_copy(u, member).start()
         guess_all[member] = guess_out[member]
-        for step in (1, 2, 3):
-            gain_copy(step).start()
-        spread_first((0, 1))
-        spread_first((2, 3))
-        spread_near((0, 1))
-        spread_far((0, 1))
-        spread_near((2, 3))
-        spread_side((0, 1), (-1, 1, 2))
-        spread_far((2, 3))
-        spread_side((2, 3), (-1, 1, 2))
+        spread_side(-1, 0)
+        spread_side(1, 1)
+        spread_far(0)
+        spread_far(1)
+        spread_near(1, 3)
+        spread_side(-1, 1)
+        spread_side(1, 0)
+        spread_near(1, 2)
+        spread_near(-1, 2)
+        spread_side(2, 0)
+        spread_side(2, 1)
+        spread_far(3)
+        spread_side(1, 3)
+        spread_near(-1, 3)
+        spread_side(1, 2)
+        spread_far(2)
+        spread_side(-1, 2)
+        spread_side(-1, 3)
+        spread_side(2, 3)
+        spread_side(2, 2)
         for step in (1, 2, 3):
             m = nth(step)
             for p in range(4):
@@ -398,20 +424,18 @@
 
         @pl.when(layer > 0)
         def _():
-            x, branch, more = exact(cin, cin_ready, last, gather_send.at[1], gather_recv.at[1], lambda: None)
+            x, branch, more = exact(cin, cin_ready, last, gather_send.at[1], gather_recv.at[1], nothing, nothing, nothing)
             out_ref[...] = (x + branch).astype(BF16).reshape(units, unit, width)
             for copy in more:
                 copy.wait_send()
 
         for copy in copies:
             copy.wait_send()
-        for copy in sent:
-            copy.wait_send()
+        for slot, p in enumerate(sent):
+            spread_copy(slot, member, mine, p, seq=sibling).wait_send()
         for step in (1, 2, 3):
             gain_copy(step).wait_send()
         for u in range(units):
-            fine_copy(u, layer + 1).wait_send()
-
             @pl.when(jnp.logical_and(u != member, layer > 0))
             def _():
                 guess_copy(u, member).wait_send()

time: 144 us -> 119 us (0.83)
  Pallas kernels: 142 us -> 117 us
    pallas_call x1, Pallas kernels: 142 us -> 117 us  [on_device(): pl.pallas_call(functools.partial(kernel, layers, seqs), out_shape=jax.Sha...]
where the time goes in v3:
time: 119 us
  Pallas kernels  117 us (98%)
  local copies, waits for them, and re-layouts  1.67 us (1%)
    pallas_call x1, Pallas kernels, on_device(): pl.pallas_call(functools.partial(kernel, layers, seqs), out_shape=jax.Sha...  117 us

profile of v3, /device:TPU:153, one launch (start us, length us, event | category | flops | bytes accessed | tf_op | source)
XLA Modules:
  0.0 118.5 jit_solution(1214294927519042876)
XLA Ops:
  0.0 116.8 %shard_map.55 = bf16[4,32,1024]{2,1,0:T(8,128)(2,1)} custom-call(bf16[4,32,1024]{2,1,0:T(8,128)(2,1)} %bitcast.8, bf16[3,4,256,512]{3,2,1,0:T(8,128)(2,1)} %bitcast.5, bf16[4,128,1024]{2,1,0:T(8,128)(2,1)} %bitcast.7, f32[1,1024]{1,0:T(1,128)} %gain_hbm.1, f32[2,64]{1,0:T(2,128)} %bitcast.9), custom_call_target="tpu_custom_call" | custom-call | tf_op jit(solution)/shard_map/pallas_call | solution.py:471
  116.8 1.7 %copy.7 = bf16[1,128,1024]{2,1,0:T(8,128)(2,1)} copy(bf16[1,128,1024]{2,1,0:T(8,128)(2,1)} %bitcast.6) | data formatting | bytes 524288

commit v4 on v3

v4 whole, which is shorter than its diff:
```python
import functools

import jax
import jax.numpy as jnp
from jax import lax
from jax.experimental import pallas as pl
from jax.experimental.pallas import tpu as pltpu
from jax.sharding import PartitionSpec as P

EPS = 1e-06
MESH = pl.DeviceIdType.MESH
F32 = jnp.float32
BF16 = jnp.bfloat16
NT = (((1,), (1,)), ((), ()))
LOG2E = 1.4426950408889634
HEAD = 64
PACK = 4
MEMBERS = 4
GROUP = 2 * MEMBERS
QUARTERS = 4
WEIGHT_PARTS = (0, 1, 2, 3)
STATE_PARTS = (4, 5, 6, 7)
ONWARD = (4, 5, 6)

FIRST_ORDER = (0, 1, 3, 2)
UNIT_ORDER = (0, 1, 3, 2)
EARLY = (("near", -1, 0), ("near", 1, 0), ("near", -1, 1), ("near", 1, 1), ("near", -1, 2), ("near", 1, 2))
LATE = (
    ("near", -1, 3), ("near", 1, 3), ("side", -1, 0), ("side", -1, 1), ("near", -1, 4), ("near", 1, 7),
    ("side", 1, 0), ("side", 1, 1), ("near", 1, 4), ("side", -1, 2), ("side", -1, 3), ("near", 1, 5),
    ("side", 1, 2), ("side", 1, 3), ("near", -1, 5), ("near", 1, 6), ("side", -1, 4), ("side", 1, 7),
    ("near", -1, 6), ("far", 2, 0), ("side", 1, 4), ("side", 1, 5), ("near", -1, 7), ("far", 2, 1),
    ("side", -1, 5), ("side", 1, 6), ("far", 2, 2), ("far", 2, 4), ("side", -1, 6), ("side", -1, 7),
    ("far", 2, 3), ("far", 2, 5), ("side", 2, 0), ("side", 2, 1), ("far", 2, 7), ("far", 2, 6),
    ("side", 2, 2), ("side", 2, 3), ("side", 2, 4), ("side", 2, 5), ("side", 2, 6), ("side", 2, 7),
)


def dot(a, b):
    return jnp.dot(a, b, preferred_element_type=F32)


def spread_queries(q, mean_square, gain):
    rows, width = q.shape
    heads = width // HEAD
    row_head = lax.broadcasted_iota(jnp.int32, (heads, rows, width), 0)
    col_head = lax.broadcasted_iota(jnp.int32, (heads, rows, width), 2) // HEAD
    spread = jnp.where(row_head == col_head, q[None], 0.0)
    head_square = jnp.sum(spread * spread, axis=-1, keepdims=True) / HEAD
    scale = lax.rsqrt(head_square + EPS * (mean_square[None] + EPS)) * (LOG2E / 8.0)
    packed = (spread * gain).astype(BF16).reshape(heads * rows, width)
    return packed, scale.reshape(heads * rows, 1)


class Mixer:
    def __init__(self, q, mean_square, gain, first_position):
        self.rows, self.width = q.shape
        self.many, self.wide = PACK * self.rows, PACK * HEAD
        self.packed, self.scale = spread_queries(q, mean_square, gain)
        self.first_position = first_position
        self.mixed = [None] * (self.width // self.wide)
        self.total = [None] * (self.width // self.wide)

    def absorb(self, columns, first_key):
        many, wide, rows = self.many, self.wide, self.rows
        for g in range(len(self.mixed)):
            these = slice(g * many, (g + 1) * many)
            keys = columns(g * wide, wide)
            tokens = keys.shape[0]
            scores = lax.dot_general(
                self.packed[these, g * wide:(g + 1) * wide], keys, NT, preferred_element_type=F32
            ) * self.scale[these]
            key_at = lax.broadcasted_iota(jnp.int32, (PACK, rows, tokens), 2).reshape(many, tokens)
            query_at = lax.broadcasted_iota(jnp.int32, (PACK, rows, tokens), 1).reshape(many, tokens)
            seen = key_at <= query_at + (self.first_position - first_key)
            weights = jnp.where(seen, jnp.exp2(scores), 0.0)
            total = sum(weights[:, i:i + 128] for i in range(0, tokens, 128))
            mixed = dot(weights.astype(BF16), columns(self.width + g * wide, wide))
            self.total[g] = total if self.total[g] is None else self.total[g] + total
            self.mixed[g] = mixed if self.mixed[g] is None else self.mixed[g] + mixed

    def result(self):
        outs = []
        for mixed, total in zip(self.mixed, self.total):
            mixed = mixed * (1.0 / jnp.sum(total, axis=-1, keepdims=True))
            mixed = mixed.reshape(PACK, self.rows, self.wide)
            row_head = lax.broadcasted_iota(jnp.int32, mixed.shape, 0)
            col_head = lax.broadcasted_iota(jnp.int32, mixed.shape, 2) // HEAD
            outs.append(jnp.sum(jnp.where(row_head == col_head, mixed, 0.0), axis=0).astype(BF16))
        return jnp.concatenate(outs, axis=-1)


def kernel(layers, seqs, x_hbm, wqkv_hbm, wo_hbm, gain_hbm, qk_hbm, out_ref,
           wq_all, wo_all, kv_all, kv_last, wkv, x_in, fine_in, cin, nxt, fine_out,
           guess_all, term_all, chain, gains_all, qk_raw, gain_raw, xs, ys,
           load, gather_send, gather_recv, spread_send, spread_recv,
           fine_send, fine_recv, guess_send, guess_recv, term_send, term_recv,
           cin_send, cin_recv, nxt_send, nxt_recv, hop_send, hop_recv, gain_send, gain_recv):
    layer = lax.axis_index("layer")
    seq = lax.axis_index("seq")
    units, unit, width = x_in.shape
    inner = width // 2
    group = layer // GROUP
    inside = lax.rem(layer, GROUP)
    member = inside // 2
    core = lax.rem(seq, 2)
    side = lax.rem(seq // 2, 2)
    even = lax.rem(layer, 2) == 0
    odd = jnp.logical_not(even)
    sibling = seq + 1 - 2 * core
    right, left = lax.rem(seq + 2, seqs), lax.rem(seq + seqs - 2, seqs)
    across = lax.rem(seq + 4, seqs)
    groups = layers // GROUP

    barrier = pltpu.get_barrier_semaphore()
    for other in (sibling, right, left):
        pl.semaphore_signal(barrier, inc=1, device_id={"seq": other}, device_id_type=MESH)
    leads = group == 0
    pair = jnp.logical_and(leads, jnp.logical_and(even, member >= 2))
    partner = 5 - member
    crossed = jnp.logical_and(group == 1, jnp.logical_and(even, member < 2))
    below = jnp.logical_and(even, group > 0)
    above = jnp.logical_and(even, group < groups - 1)

    def greet(when, other):
        @pl.when(when)
        def _():
            pl.semaphore_signal(barrier, inc=1, device_id={"layer": other}, device_id_type=MESH)

    for step in range(1, GROUP):
        other = group * GROUP + lax.rem(inside + step, GROUP)
        greet(jnp.logical_or(even, lax.rem(inside + step, 2) == 0), other)
    greet(below, layer - GROUP)
    greet(above, layer + GROUP)
    greet(pair, GROUP + 2 * (3 - member))
    greet(crossed, 2 * (3 - member))

    def count(when, amount):
        return jnp.where(when, amount, 0)

    greeted = (3 + jnp.where(even, GROUP - 1, MEMBERS) + count(below, 1) + count(above, 1) + count(crossed, 1)
               + count(pair, 1))

    loads = [
        pltpu.make_async_copy(x_hbm, x_in, load.at[0]),
        pltpu.make_async_copy(gain_hbm, gain_raw, load.at[1]),
        pltpu.make_async_copy(qk_hbm, qk_raw, load.at[2]),
        pltpu.make_async_copy(wqkv_hbm.at[1], wkv.at[0], load.at[3]),
        pltpu.make_async_copy(wqkv_hbm.at[2], wkv.at[1], load.at[4]),
        pltpu.make_async_copy(wqkv_hbm.at[0], wq_all.at[member], load.at[5]),
        pltpu.make_async_copy(wo_hbm, wo_all.at[member], load.at[6]),
    ]
    for copy in loads:
        copy.start()
    for copy in loads[:3]:
        copy.wait()
    gains_all[member, 0:1, :] = gain_raw[...]
    gains_all[member, 1:2, :] = jnp.concatenate([qk_raw[0:1, :]] * (inner // HEAD) + [qk_raw[1:2, :]] * (inner // HEAD), axis=-1)
    for copy in loads[3:]:
        copy.wait()
    norm_gain = gains_all[member, 0:1, :]
    query_gain = gains_all[member, 1:2, 0:inner]
    key_gain = gains_all[member, 1:2, inner:width]

    def remote(src, dst, send, recv, **target):
        return pltpu.make_async_remote_copy(
            src_ref=src, dst_ref=dst, send_sem=send, recv_sem=recv, device_id=target, device_id_type=MESH)

    def member_layer(m):
        return group * GROUP + 2 * m

    mine, others = 2 * side + core, 2 * (1 - side) + core

    def nth(step):
        return lax.rem(member + step + MEMBERS, MEMBERS)

    def part(m, quarter, p):
        if p in STATE_PARTS:
            p = p - STATE_PARTS[0]
            return kv_all.at[m, 2 * quarter + p // 2].at[pl.ds((p % 2) * (2 * unit), 2 * unit)]
        ref = (wq_all if p < 2 else wo_all).at[m, quarter]
        rows = ref.shape[0] // 2
        return ref.at[pl.ds((p % 2) * rows, rows)]

    def spread_copy(slot, m, quarter, p, **target):
        ref = part(m, quarter, p)
        return remote(ref, ref, spread_send.at[slot], spread_recv.at[m, quarter, p], **target)

    def hand(m, quarter, p, book=None, **target):
        book = sent if book is None else book
        spread_copy(len(book), m, quarter, p, **target).start()
        book.append(p)

    def await_part(m, quarter, p):
        spread_copy(0, m, quarter, p, seq=sibling).wait_recv()

    def spread_first(step, parts):
        for p in parts:
            hand(member, mine, p, layer=member_layer(nth(step)))

    def spread_on(moves):
        for kind, step, p in moves:
            m = nth(step)
            quarter = others if kind == "side" else mine
            await_part(m, quarter, p)
            if kind == "near" and (step == -1) == (p in ONWARD):
                hand(m, mine, p, layer=member_layer(nth(-step)))
            if kind != "side":
                hand(m, mine, p, seq=right if p % 2 == 0 else left)
            hand(m, quarter, p, seq=sibling)

    def spread_end(m):
        for p in WEIGHT_PARTS + STATE_PARTS:
            await_part(m, 2 * side + 1 - core, p)
            await_part(m, 2 * (1 - side) + 1 - core, p)

    def pair_first(parts):
        for p in parts:
            hand(member, mine, p, pair_sent, layer=member_layer(partner))

    def pair_near(parts):
        for p in parts:
            await_part(partner, mine, p)
            hand(partner, mine, p, pair_sent, seq=right if p % 2 == 0 else left)
            hand(partner, mine, p, pair_sent, seq=sibling)

    def pair_side(parts):
        for p in parts:
            await_part(partner, others, p)
            hand(partner, others, p, pair_sent, seq=sibling)

    def spread_drain(book):
        for slot, p in enumerate(book):
            spread_copy(slot, member, mine, p, seq=sibling).wait_send()

    later = jnp.logical_and(even, group > 0)
    sent, pair_sent = [], []

    def exact(source, ready, first, kv, send, recv, meet, pushed, gathered):
        copies = []
        order = [lax.rem(first + i, MEMBERS) if not isinstance(first, int) else i for i in UNIT_ORDER]

        def at(block, u):
            return kv(block).at[pl.ds(u * unit, unit)]

        def push(block, u, target):
            copy = remote(at(block, u), at(block, u), send.at[len(copies)], recv.at[block, u], seq=target)
            copy.start()
            copies.append(copy)

        def arrived(block, u):
            remote(at(block, u), at(block, u), send.at[0], recv.at[block, u], seq=sibling).wait_recv()

        same = lax.broadcasted_iota(jnp.int32, (inner, inner), 0) // HEAD
        same = (same == lax.broadcasted_iota(jnp.int32, (inner, inner), 1) // HEAD).astype(BF16)
        for k, u in enumerate(order):
            ready(u)
            here = pl.ds(u * unit, unit)
            x = source[u].astype(F32)
            xs[here, :] = x
            mean_square = jnp.mean(x * x, axis=-1, keepdims=True)
            y = (x * norm_gain).astype(BF16)
            ys[here, :] = y
            key = dot(y, wkv[0].reshape(width, inner))
            head_square = dot((key * key).astype(BF16), same) / HEAD
            key = key * lax.rsqrt(head_square + EPS * (mean_square + EPS)) * key_gain
            at(seq, u)[:, 0:inner] = key.astype(BF16)
            value = dot(y, wkv[1].reshape(width, inner)) * lax.rsqrt(mean_square + EPS)
            at(seq, u)[:, inner:width] = value.astype(BF16)
            if k == 0:
                meet()
            push(seq, u, right)
            push(seq, u, left)
            push(seq, u, sibling)
        pushed()
        x = xs[...]
        mean_square = jnp.mean(x * x, axis=-1, keepdims=True)
        q = dot(ys[...], wq_all[member].reshape(width, inner))
        mixer = Mixer(q, mean_square, query_gain, seq * units * unit)

        def absorb(block):
            chip = block // 2

            def columns(start, size):
                return kv(pl.ds(2 * chip, 2))[:, :, start:start + size].reshape(2 * units * unit, size)

            mixer.absorb(columns, chip * (2 * units * unit))

        for u in order:
            arrived(sibling, u)
        absorb(seq)
        for k, u in enumerate(order):
            arrived(left, u)
            if k % 2 == 0:
                push(left, u, right)
            push(left, u, sibling)
            arrived(right, u)
            if k % 2 == 1:
                push(right, u, left)
            push(right, u, sibling)
        for side_block, step in ((left, seqs - 2), (right, 2)):
            for u in order:
                arrived(lax.rem(sibling + step, seqs), u)
            absorb(side_block)
        for u in order:
            arrived(across, u)
            push(across, u, sibling)
        for u in order:
            arrived(lax.rem(sibling + 4, seqs), u)
        gathered()
        absorb(across)
        branch = dot(mixer.result(), wo_all[member].reshape(inner, width))
        return x, branch, copies

    def held(block):
        return kv_all.at[member, block]

    def last(block):
        return kv_last.at[block]

    def fine_copy(u, target):
        return remote(fine_out.at[u], fine_in.at[u], fine_send.at[u], fine_recv.at[u], layer=target)

    @pl.when(even)
    def _():
        for u in range(units):
            fine_in[u] = x_in[u]

    def fine_ready(u):
        @pl.when(odd)
        def _():
            if u == UNIT_ORDER[0]:
                pl.semaphore_wait(barrier, greeted)
            fine_copy(u, layer - 1).wait_recv()

    def meet():
        @pl.when(even)
        def _():
            pl.semaphore_wait(barrier, greeted)

    def pushed():
        @pl.when(later)
        def _():
            spread_first(1, WEIGHT_PARTS)
            spread_first(-1, WEIGHT_PARTS)
            for step in (1, 2, 3):
                gain_copy(step).start()

        @pl.when(pair)
        def _():
            pair_first(WEIGHT_PARTS)
            gain_to(partner, 0).start()

    def gathered():
        @pl.when(later)
        def _():
            spread_first(-1, (7, 4, 5, 6))
            spread_first(1, (4,))
            spread_on(EARLY)

    def nothing():
        pass

    def gain_to(m, slot):
        ref = gains_all.at[member]
        return remote(ref, ref, gain_send.at[slot], gain_recv.at[member], layer=member_layer(m))

    def gain_copy(step):
        return gain_to(nth(step), step - 1)

    x, branch, copies = exact(fine_in, fine_ready, 0, held, gather_send.at[0], gather_recv.at[0], meet, pushed, gathered)
    fine_out[...] = (x + branch).astype(BF16).reshape(units, unit, width)

    def pair_home(u):
        return 2 if u in (1, 2) else 3

    def home(u):
        first = jnp.where(inside < 4, 2, 2 * pair_home(u))
        return jnp.where(leads, first, group * GROUP + 2 * u)

    def guess_copy(u):
        ref = guess_all.at[member, u]
        return remote(ref, ref, guess_send.at[u], guess_recv.at[member, u], layer=home(u))

    def term_copy(u):
        return remote(fine_out.at[u], term_all.at[member, u], term_send.at[u], term_recv.at[member, u], layer=home(u))

    def start_copy(u):
        return remote(fine_out.at[u], chain.at[1, u], term_send.at[u], hop_recv.at[u], layer=layer + 1)

    def guess_goes(u):
        return jnp.logical_or(jnp.logical_and(later, u != member), jnp.logical_and(pair, pair_home(u) != member))

    @pl.when(odd)
    def _():
        @pl.when(layer == 1)
        def _():
            for u in FIRST_ORDER:
                start_copy(u).start()
            out_ref[...] = fine_out[...]

        @pl.when(layer > 1)
        def _():
            for u in range(units):
                term_copy(u).start()

        for copy in copies:
            copy.wait_send()
        for u in range(units):
            term_copy(u).wait_send()

        @pl.when(layer > 1)
        def _():
            for u in range(units):
                remote(chain.at[0, 0], nxt.at[u], nxt_send.at[0, 0], nxt_recv.at[u], layer=layer - 1).wait_recv()
            out_ref[...] = nxt[...]

    def cin_copy(m, u):
        return remote(chain.at[m, u], cin.at[u], cin_send.at[m, u], cin_recv.at[u], layer=member_layer(m))

    def nxt_copy(m, u):
        return remote(chain.at[m + 1, u], nxt.at[u], nxt_send.at[m, u], nxt_recv.at[u], layer=member_layer(m) + 1)

    def hop_copy(u, target):
        return remote(chain.at[MEMBERS, u], chain.at[0, u], hop_send.at[u], hop_recv.at[u], layer=target)

    def guess_wait(m, u):
        ref = guess_all.at[m, u]
        remote(ref, ref, guess_send.at[0], guess_recv.at[m, u], layer=layer + 1).wait_recv()

    def term_wait(m, u):
        ref = term_all.at[m, u]
        remote(ref, ref, term_send.at[0], term_recv.at[m, u], layer=layer + 1).wait_recv()

    def gain_wait(m):
        remote(gains_all.at[m], gains_all.at[m], gain_send.at[0], gain_recv.at[m], seq=sibling).wait_recv()

    def coarse_step(m, rows, correction, first_position):
        x = rows.astype(F32)
        mean_square = jnp.mean(x * x, axis=-1, keepdims=True)
        q = dot((x * gains_all[m, 0:1, :]).astype(BF16), wq_all[m].reshape(width, inner))

        def columns(start, size):
            return kv_all[m, :, :, start:start + size].reshape(seqs * units * unit, size)

        mixer = Mixer(q, mean_square, gains_all[m, 1:2, 0:inner], first_position)
        mixer.absorb(columns, 0)
        return (x + 2.0 * dot(mixer.result(), wo_all[m].reshape(inner, width)) + correction).astype(BF16)

    @pl.when(even)
    def _():
        for u in UNIT_ORDER:
            fine_copy(u, layer + 1).start()
        guess_all[member] = (x + 2.0 * branch).astype(BF16).reshape(units, unit, width)

    @pl.when(later)
    def _():
        spread_first(1, (5, 6, 7))

    @pl.when(pair)
    def _():
        pair_first(STATE_PARTS)
        pair_near((0, 1, 2))

    for u in range(units):
        @pl.when(guess_goes(u))
        def _():
            guess_copy(u).start()

    def hop_arrives(u):
        hop_copy(u, layer - 1).wait_recv()

    def lead_copy(u):
        return remote(chain.at[2, u], chain.at[2, u], hop_send.at[u], hop_recv.at[u], layer=2 * pair_home(u))

    def lead_nxt(u):
        return remote(chain.at[2, u], nxt.at[u], nxt_send.at[1, u], nxt_recv.at[u], layer=layer + 1)

    def step_one(m, u):
        term_wait(m, u)
        correction = term_all[m, u].astype(F32) - guess_all[m, u].astype(F32)
        chain[m + 1, u] = coarse_step(m, chain[m, u], correction, (seq * units + u) * unit)

    @pl.when(layer == 2)
    def _():
        for u in FIRST_ORDER:
            hop_arrives(u)
            step_one(1, u)
            lead_copy(u).start()
            lead_nxt(u).start()
        cin[...] = chain[1]

    def pair_units(body):
        for m in (2, 3):
            @pl.when(member == m)
            def _():
                for u in FIRST_ORDER:
                    if pair_home(u) == m:
                        body(m, u)

    @pl.when(pair)
    def _():
        pair_near((3,))
        pair_side((0, 1, 2))
        pair_near((4,))
        pair_side((3,))
        pair_near((5, 6))
        pair_side((4,))
        pair_near((7,))
        pair_side((5, 6, 7))
        spread_end(partner)
        gain_wait(partner)

        def walk(mine_m, u):
            hop_arrives(u)
            if mine_m == 2:
                cin[u] = chain[2, u]
            else:
                cin_copy(2, u).start()
                guess_wait(2, u)
            step_one(2, u)
            if mine_m == 3:
                cin[u] = chain[3, u]
            else:
                cin_copy(3, u).start()
                guess_wait(3, u)
            step_one(3, u)
            hop_copy(u, GROUP + 2 * u).start()
            nxt_copy(2, u).start()
            nxt_copy(3, u).start()

        pair_units(walk)

    @pl.when(later)
    def _():
        spread_on(LATE)
        for step in (-1, 1, 2):
            spread_end(nth(step))
        for step in (1, 2, 3):
            gain_wait(nth(step))
        hop_copy(member, layer - GROUP).wait_recv()

        def advance(m, carry):
            @pl.when(m != member)
            def _():
                cin_copy(m, member).start()
                guess_wait(m, member)

            @pl.when(m == member)
            def _():
                cin[member] = chain[m, member]

            term_wait(m, member)
            correction = term_all[m, member].astype(F32) - guess_all[m, member].astype(F32)
            chain[m + 1, member] = coarse_step(m, chain[m, member], correction, (seq * units + member) * unit)

            @pl.when(jnp.logical_and(m == MEMBERS - 1, group < groups - 1))
            def _():
                hop_copy(member, layer + GROUP).start()

            nxt_copy(m, member).start()
            return carry

        lax.fori_loop(0, MEMBERS, advance, 0)

    def cin_comes(u):
        in_pair = jnp.logical_or(u == 1, u == 2)
        from_other = jnp.logical_or(jnp.logical_and(in_pair, member == 3), jnp.logical_and(jnp.logical_not(in_pair), member == 2))
        return jnp.logical_or(jnp.logical_and(later, u != member), jnp.logical_and(pair, from_other))

    def cin_ready(u):
        @pl.when(cin_comes(u))
        def _():
            remote(chain.at[0, 0], cin.at[u], cin_send.at[0, 0], cin_recv.at[u], layer=layer + 1).wait_recv()

    @pl.when(layer == 0)
    def _():
        out_ref[...] = fine_out[...]

    @pl.when(jnp.logical_and(even, layer > 0))
    def _():
        x, branch, more = exact(cin, cin_ready, member, last, gather_send.at[1], gather_recv.at[1], nothing, nothing, nothing)
        out_ref[...] = (x + branch).astype(BF16).reshape(units, unit, width)
        for copy in more:
            copy.wait_send()

    @pl.when(even)
    def _():
        for u in range(units):
            fine_copy(u, layer + 1).wait_send()
        for copy in copies:
            copy.wait_send()

    for u in range(units):
        @pl.when(guess_goes(u))
        def _():
            guess_copy(u).wait_send()

    @pl.when(layer == 2)
    def _():
        for u in range(units):
            lead_copy(u).wait_send()
            lead_nxt(u).wait_send()

    @pl.when(pair)
    def _():
        spread_drain(pair_sent)
        gain_to(partner, 0).wait_send()

        def drained(mine_m, u):
            cin_copy(5 - mine_m, u).wait_send()
            hop_copy(u, GROUP + 2 * u).wait_send()
            nxt_copy(2, u).wait_send()
            nxt_copy(3, u).wait_send()

        pair_units(drained)

    @pl.when(later)
    def _():
        spread_drain(sent)
        for step in (1, 2, 3):
            gain_copy(step).wait_send()

        def drain(m, carry):
            nxt_copy(m, member).wait_send()

            @pl.when(m != member)
            def _():
                cin_copy(m, member).wait_send()

            return carry

        lax.fori_loop(0, MEMBERS, drain, 0)

        @pl.when(group < groups - 1)
        def _():
            hop_copy(member, layer + GROUP).wait_send()


def solution(mesh):
    layers, seqs = mesh.shape["layer"], mesh.shape["seq"]

    def on_device(states, w_qkv, w_out, norm_gain, qk_gain):
        rows, width = states.shape[1:]
        inner = w_out.shape[1]
        unit = rows // MEMBERS
        hbm = pl.BlockSpec(memory_space=pl.ANY)
        dma = pltpu.SemaphoreType.DMA
        state = pltpu.VMEM((MEMBERS, unit, width), BF16)
        rows_of = pltpu.VMEM((MEMBERS, MEMBERS, unit, width), BF16)
        out = pl.pallas_call(
            functools.partial(kernel, layers, seqs),
            out_shape=jax.ShapeDtypeStruct((MEMBERS, unit, width), BF16),
            in_specs=[hbm] * 5,
            out_specs=pl.BlockSpec(memory_space=pltpu.VMEM),
            scratch_shapes=[
                pltpu.VMEM((MEMBERS, QUARTERS, width // QUARTERS, inner), BF16),
                pltpu.VMEM((MEMBERS, QUARTERS, inner // QUARTERS, width), BF16),
                pltpu.VMEM((MEMBERS, seqs, rows, 2 * inner), BF16),
                pltpu.VMEM((seqs, rows, 2 * inner), BF16),
                pltpu.VMEM((2, QUARTERS, width // QUARTERS, inner), BF16),
                state, state, state, state, state, rows_of, rows_of,
                pltpu.VMEM((MEMBERS + 1, MEMBERS, unit, width), BF16),
                pltpu.VMEM((MEMBERS, 8, width), F32),
                pltpu.VMEM((2, HEAD), F32),
                pltpu.VMEM((1, width), F32),
                pltpu.VMEM((rows, width), F32),
                pltpu.VMEM((rows, width), BF16),
                dma((7,)), dma((2, 28)), dma((2, seqs, MEMBERS)), dma((96,)), dma((MEMBERS, QUARTERS, 8)),
                dma((4,)), dma((4,)), dma((4,)), dma((4, 4)), dma((4,)), dma((4, 4)),
                dma((4, 4)), dma((4,)), dma((4, 4)), dma((4,)), dma((4,)), dma((4,)), dma((3,)), dma((4,)),
            ],
            compiler_params=pltpu.CompilerParams(
                collective_id=0, has_side_effects=True, vmem_limit_bytes=56 << 20),
        )(
            states.reshape(MEMBERS, unit, width),
            w_qkv.reshape(3, QUARTERS, width // QUARTERS, inner),
            w_out.reshape(QUARTERS, inner // QUARTERS, width),
            norm_gain, qk_gain[0],
        )
        return out.reshape(1, rows, width)

    in_specs = (
        P("layer", "seq", None),
        P("layer", None, None, None),
        P("layer", None, None),
        P("layer", None),
        P("layer", None, None),
    )
    return jax.shard_map(
        on_device, mesh=mesh, in_specs=in_specs, out_specs=P("layer", "seq", None), check_vma=False
    )
```

time: 119 us -> 104 us (0.87)
  Pallas kernels: 117 us -> 101 us
    pallas_call x1, Pallas kernels: 117 us -> 101 us  [on_device(): pl.pallas_call(functools.partial(kernel, layers, seqs), out_shape=jax.Sha...]
where the time goes in v4:
time: 104 us; the launch traced here: 103 us
  Pallas kernels  101 us (97%)
  local copies, waits for them, and re-layouts  1.67 us (2%)
    pallas_call x1, Pallas kernels, on_device(): pl.pallas_call(functools.partial(kernel, layers, seqs), out_shape=jax.Sha...  101 us

profile of v4, /device:TPU:153, one launch (start us, length us, event | category | flops | bytes accessed | tf_op | source)
XLA Modules:
  0.0 102.8 jit_solution(18045328704881878174)
XLA Ops:
  0.0 101.2 %shard_map.55 = bf16[4,32,1024]{2,1,0:T(8,128)(2,1)} custom-call(bf16[4,32,1024]{2,1,0:T(8,128)(2,1)} %bitcast.8, bf16[3,4,256,512]{3,2,1,0:T(8,128)(2,1)} %bitcast.5, bf16[4,128,1024]{2,1,0:T(8,128)(2,1)} %bitcast.7, f32[1,1024]{1,0:T(1,128)} %gain_hbm.1, f32[2,64]{1,0:T(2,128)} %bitcast.9), custom_call_target="tpu_custom_call" | custom-call | tf_op jit(solution)/shard_map/pallas_call | solution.py:651
  101.2 1.7 %copy.7 = bf16[1,128,1024]{2,1,0:T(8,128)(2,1)} copy(bf16[1,128,1024]{2,1,0:T(8,128)(2,1)} %bitcast.6) | data formatting | bytes 524288

commit v5 on v4

--- a/solution.py
+++ b/solution.py
@@ -401,7 +401,7 @@
 
         @pl.when(layer > 1)
         def _():
-            for u in range(units):
+            for u in FIRST_ORDER:
                 term_copy(u).start()
 
         for copy in copies:

time: 104 us -> 104 us (level)
  no operation moved by 1% of the time
where the time goes in v5:
time: 104 us; the launch traced here: 103 us
  Pallas kernels  101 us (97%)
  local copies, waits for them, and re-layouts  1.67 us (2%)
    pallas_call x1, Pallas kernels, on_device(): pl.pallas_call(functools.partial(kernel, layers, seqs), out_shape=jax.Sha...  101 us

profile of v5, /device:TPU:153, one launch (start us, length us, event | category | flops | bytes accessed | tf_op | source)
XLA Modules:
  0.0 102.8 jit_solution(10354622577547417885)
XLA Ops:
  0.0 101.2 %shard_map.55 = bf16[4,32,1024]{2,1,0:T(8,128)(2,1)} custom-call(bf16[4,32,1024]{2,1,0:T(8,128)(2,1)} %bitcast.8, bf16[3,4,256,512]{3,2,1,0:T(8,128)(2,1)} %bitcast.5, bf16[4,128,1024]{2,1,0:T(8,128)(2,1)} %bitcast.7, f32[1,1024]{1,0:T(1,128)} %gain_hbm.1, f32[2,64]{1,0:T(2,128)} %bitcast.9), custom_call_target="tpu_custom_call" | custom-call | tf_op jit(solution)/shard_map/pallas_call | solution.py:651
  101.2 1.7 %copy.7 = bf16[1,128,1024]{2,1,0:T(8,128)(2,1)} copy(bf16[1,128,1024]{2,1,0:T(8,128)(2,1)} %bitcast.6) | data formatting | bytes 524288
